TPU v7x, 128 devices: a whole 4x4x4 slice. The times are simulated.
128 devices in a mesh: row: 4 (over x), col: 32 (over z, y, core).
Axes of the slice: x: 4, y: 4, z: 4, core: 2. Of those that a mesh axis runs over, the one named last changes fastest.
Arguments:
- tokens: bfloat16 [112, 896, 768], P('row', 'col'), may hold values from -6 to 6
- project_in: bfloat16 [768, 2304], replicated, may hold values from -8 to 8
- project_out: bfloat16 [768, 768], replicated, may hold values from -0.21875 to 0.21875
- expand_weight: bfloat16 [768, 3072], replicated, may hold values from -0.21875 to 0.21875
- reduce_weight: bfloat16 [3072, 768], replicated, may hold values from -0.109375 to 0.109375
- first_weight: bfloat16 [49, 768, 1024], P(None, 'row', 'col'), may hold values from -0.03125 to 0.03125
- first_bias: float32 [1024], replicated, may hold values from -3 to 3
- second_weight: bfloat16 [1024, 1024], replicated, may hold values from -0.1875 to 0.1875
- second_bias: float32 [1024], replicated, may hold values from -3 to 3
- box_tile: int32 [4096, 1], replicated, may hold values from 0 to 127; in each aligned block of 128 rows (0 to 127, 128 to 255, ...) at most 2 rows name the same one
- box_shape: int32 [4096, 4], replicated, may hold values from 0 to 7, as said below
Outputs:
- features: bfloat16 [112, 896, 768], P('row', 'col')
- box_features: bfloat16 [4096, 1024], P('col', 'row')
Inputs may be any that keep to these rules, and one draw needn't show every extreme that they name: `box_tile`: among the 128 boxes of one aligned block (boxes b * 128 to (b + 1) * 128 - 1), no tile is named more than 2 times, a bound that some block reaches; every tile holds some box. `box_shape`: steps are 1 or 2, and first + 6 step < 14 in both directions, so all samples of a box lie in its tile.
All inputs are finite; a program needn't handle non-finite values.
Results may differ from a plain program's by a relative error of at most 0.02.
Values may be sent and summed in bfloat16 or wider, within the bound.
A program may use at most 192 MiB of HBM per device.

v0:
```python
import jax
import jax.numpy as jnp
from jax import lax
from jax.sharding import PartitionSpec as P

HEADS = 12
WIN = 14
POOL = 7


eps = 1e-06
masked = -1e30


def padded(cells, sides, width):
    for axis, dim in sides:
        count = lax.axis_size(axis)
        ends = count - 1
        head = lax.slice_in_dim(cells, 0, width, axis=dim)
        tail = lax.slice_in_dim(cells, cells.shape[dim] - width, cells.shape[dim], axis=dim)
        cells = jnp.concatenate(
            [
                lax.ppermute(tail, axis, [(i, (i + 1) % count) for i in range(ends)]),
                cells,
                lax.ppermute(head, axis, [((i + 1) % count, i) for i in range(ends)]),
            ],
            axis=dim,
        )
    return cells


def layer_norm(values):
    values = values.astype(jnp.float32)
    center = values - jnp.mean(values, axis=-1, keepdims=True)
    spread = jnp.mean(center * center, axis=-1, keepdims=True)
    return (center * lax.rsqrt(spread + eps)).astype(jnp.bfloat16)


def to_windows(lattice, window):
    side_rows, side_cols, channels = lattice.shape
    row_blocks = side_rows // window
    col_blocks = side_cols // window
    shaped = lattice.reshape(row_blocks, window, col_blocks, window, channels)
    return shaped.transpose(0, 2, 1, 3, 4).reshape(
        row_blocks * col_blocks, window * window, channels
    )


def from_windows(blocks, row_blocks, col_blocks, window):
    channels = blocks.shape[-1]
    shaped = blocks.reshape(row_blocks, col_blocks, window, window, channels)
    return shaped.transpose(0, 2, 1, 3, 4).reshape(
        row_blocks * window, col_blocks * window, channels
    )


def attend(queries, key_value, inside, head_count):
    window_count, length, width_all = queries.shape
    head_size = width_all // head_count
    query_heads = queries.reshape(window_count, length, head_count, head_size)
    key_heads = key_value[..., :width_all].reshape(window_count, length, head_count, head_size)
    value_heads = key_value[..., width_all:].reshape(window_count, length, head_count, head_size)
    scores = jnp.einsum(
        "nqhd,nkhd->nhqk", query_heads, key_heads, preferred_element_type=jnp.float32
    ) * head_size ** (-0.5)
    scores = jnp.where(inside[:, None, None, :], scores, masked)
    row_max = jnp.max(scores, axis=-1, keepdims=True)
    weights = jnp.exp(scores - row_max)
    shares = (weights / jnp.sum(weights, axis=-1, keepdims=True)).astype(jnp.bfloat16)
    blended = jnp.einsum("nhqk,nkhd->nqhd", shares, value_heads, preferred_element_type=jnp.float32)
    return blended.reshape(window_count, length, width_all).astype(jnp.bfloat16)


def finish(tokens_flat, blended, project_out, expand_weight, reduce_weight):
    after_attention = tokens_flat.astype(jnp.float32) + jnp.dot(
        blended, project_out, preferred_element_type=jnp.float32
    )
    hidden = jax.nn.gelu(
        jnp.dot(layer_norm(after_attention), expand_weight, preferred_element_type=jnp.float32)
    ).astype(jnp.bfloat16)
    return (
        after_attention + jnp.dot(hidden, reduce_weight, preferred_element_type=jnp.float32)
    ).astype(jnp.bfloat16)


def shards(
    tokens,
    project_in,
    project_out,
    expand_weight,
    reduce_weight,
    first_weight,
    first_bias,
    second_weight,
    second_bias,
    box_tile,
    box_shape,
):
    margin = WIN // 2
    row_count = lax.axis_size("row")
    col_count = lax.axis_size("col")
    row_pos = lax.axis_index("row")
    col_pos = lax.axis_index("col")
    tile_side = tokens.shape[0]
    model_width = tokens.shape[2]
    padded_side = tile_side + 2 * margin
    normed = layer_norm(tokens.reshape(-1, model_width))
    queries = jnp.dot(
        normed, project_in[:, :model_width], preferred_element_type=jnp.float32
    ).astype(jnp.bfloat16)
    queries = queries.reshape(tile_side, tile_side, model_width)
    rimmed = padded(tokens, (("row", 0), ("col", 1)), margin)
    key_value = jnp.dot(
        layer_norm(rimmed.reshape(-1, model_width)),
        project_in[:, model_width:],
        preferred_element_type=jnp.float32,
    ).astype(jnp.bfloat16)
    key_value = key_value.reshape(padded_side, padded_side, 2 * model_width)
    queries = jnp.pad(queries, ((margin, margin), (margin, margin), (0, 0)))
    offsets = jnp.arange(padded_side, dtype=jnp.int32) - margin
    row_coord = row_pos * tile_side + offsets
    col_coord = col_pos * tile_side + offsets
    row_inside = (row_coord >= 0) & (row_coord < tile_side * row_count)
    col_inside = (col_coord >= 0) & (col_coord < tile_side * col_count)
    inside = row_inside[:, None] & col_inside[None, :]
    blocks_side = padded_side // WIN
    blended = attend(
        to_windows(queries, WIN),
        to_windows(key_value, WIN),
        to_windows(inside[:, :, None], WIN)[..., 0],
        HEADS,
    )
    blended = from_windows(blended, blocks_side, blocks_side, WIN)[
        margin : margin + tile_side, margin : margin + tile_side
    ]
    features = finish(
        tokens.reshape(-1, model_width),
        blended.reshape(-1, model_width),
        project_out,
        expand_weight,
        reduce_weight,
    )
    features = features.reshape(tile_side, tile_side, model_width)
    half_side = tile_side // 2
    pooled = (
        features.astype(jnp.float32)
        .reshape(half_side, 2, half_side, 2, model_width)
        .sum(axis=(1, 3))
        * 0.25
    ).astype(jnp.bfloat16)
    group_width = model_width // row_count
    grouped = pooled.reshape(half_side * half_side, row_count, group_width).transpose(1, 0, 2)
    anchors = box_tile[:, 0].reshape(col_count, -1)
    per_col = anchors.shape[1]
    capacity = 2 * per_col // (row_count * col_count)
    own_tile = row_pos * col_count + col_pos
    at_home = (anchors == own_tile).astype(jnp.int32)
    ranking = jnp.cumsum(at_home, axis=1) - 1
    slot_numbers = jnp.arange(capacity, dtype=jnp.int32)
    selector = at_home[:, None, :] * (ranking[:, None, :] == slot_numbers[None, :, None]).astype(
        jnp.int32
    )
    geometry = box_shape.reshape(col_count, per_col, 4)
    chosen = jnp.sum(selector[..., None] * geometry[:, None, :, :], axis=2)
    pool_steps = jnp.arange(POOL, dtype=jnp.int32)
    sample_rows = chosen[..., 0:1] + pool_steps * chosen[..., 2:3]
    sample_cols = chosen[..., 1:2] + pool_steps * chosen[..., 3:4]
    sample_at = (sample_rows[..., :, None] * half_side + sample_cols[..., None, :]).reshape(-1)
    gathered = jnp.take(grouped, sample_at, axis=1)
    bin_count = POOL * POOL
    outgoing = gathered.reshape(row_count * col_count, capacity, bin_count, group_width)
    received = lax.all_to_all(outgoing, ("row", "col"), split_axis=0, concat_axis=0, tiled=True)
    received = received.reshape(row_count * col_count * capacity, bin_count, group_width)
    own_tiles = lax.dynamic_slice_in_dim(box_tile[:, 0], col_pos * per_col, per_col)
    positions = jnp.arange(per_col, dtype=jnp.int32)
    earlier = positions[:, None] < positions[None, :]
    matching = (own_tiles[:, None] == own_tiles[None, :]) & earlier
    rank_own = jnp.sum(matching.astype(jnp.int32), axis=0)
    own_crops = jnp.take(received, own_tiles * capacity + rank_own, axis=0)
    first_sum = lax.dot_general(
        own_crops,
        lax.all_gather(first_weight, "col", axis=2, tiled=True),
        (((1, 2), (0, 1)), ((), ())),
        preferred_element_type=jnp.float32,
    )
    unit_share = first_bias.shape[0] // row_count
    first_share = lax.psum_scatter(
        first_sum.astype(jnp.bfloat16), "row", scatter_dimension=1, tiled=True
    ).astype(jnp.float32)
    bias_share = lax.dynamic_slice_in_dim(first_bias, row_pos * unit_share, unit_share, 0)
    box_hidden = jax.nn.relu(first_share + bias_share).astype(jnp.bfloat16)
    second_rows = lax.dynamic_slice_in_dim(second_weight, row_pos * unit_share, unit_share, 0)
    second_part = jnp.dot(box_hidden, second_rows, preferred_element_type=jnp.float32)
    second_sum = lax.psum_scatter(
        second_part.astype(jnp.bfloat16), "row", scatter_dimension=1, tiled=True
    ).astype(jnp.float32)
    second_bias_share = lax.dynamic_slice_in_dim(second_bias, row_pos * unit_share, unit_share, 0)
    box_features = jax.nn.relu(second_sum + second_bias_share).astype(jnp.bfloat16)
    return (features, box_features)


def solution(mesh):
    return jax.shard_map(
        shards,
        mesh=mesh,
        in_specs=(
            P("row", "col", None),
            P(),
            P(),
            P(),
            P(),
            P(None, "row", "col"),
            P(),
            P(),
            P(),
            P(),
            P(),
        ),
        out_specs=(P("row", "col", None), P("col", "row")),
        check_vma=False,
    )
```

profile of v0, /device:TPU:0, one launch (start us, length us, event | category | flops | bytes accessed | tf_op | source)
XLA Modules:
  0.0 488.7 jit_solution(16519496756893991516)
XLA Ops:
  7.9 2.0 fusion.65
  9.9 4.2 collective-permute-start
  15.4 3.1 reshape.265
  25.6 4.2 convolution_convert_fusion.1
  29.9 1.8 add.238
  32.8 3.0 reshape.258
  35.8 3.7 pad.4
  39.6 5.3 %reshape.259 = bf16[3,14,3,14,768]{4,3,2,1,0:T(8,128)(2,1)} reshape(bf16[42,42,768]{2,1,0:T(8,128)(2,1)} %pad.4) | data formatting | bytes 5419008 | tf_op jit(solution)/shard_map/reshape | solution.py:43
  44.9 3.9 copy.89
  48.8 9.7 %reshape_reshape.7 = bf16[9,196,12,64]{3,2,1,0:T(8,128)(2,1)} reshape(bf16[3,3,14,14,768]{4,3,2,1,0:T(8,128)(2,1)} %copy.89) | data formatting | bytes 5419008 | tf_op jit(solution)/shard_map/reshape;reshape | solution.py:60
  66.4 3.9 collective-permute-done.3
  70.4 2.9 fusion.62
  73.4 3.7 multiply_reduce_fusion
  77.2 5.4 %maximum_convert_fusion = f32[42,42,768]{2,1,0:T(8,128)} fusion(bf16[42,7,768]{2,1,0:T(8,128)(2,1)S(1)} %collective-permute-done.3, bf16[42,28,768]{2,1,0:T(8,128)(2,1)} %copy-done.2, bf16[42,7,768]{2,1,0:T(8,128)(2,1)S(1)} %collective-permute-done.2), kind=kLoop, calls=%fused_computation.32 | loop fusion | flops 8128512 | bytes 8128512 | tf_op jit(solution)/shard_map/convert_element_type | solution.py:33
  82.6 7.1 %reshape.266 = f32[1764,768]{1,0:T(8,128)} reshape(f32[42,42,768]{2,1,0:T(8,128)} %maximum_convert_fusion) | data formatting | bytes 10838016 | tf_op jit(solution)/shard_map/convert_element_type | solution.py:33
  89.7 10.2 %convolution_convert_fusion = bf16[1764,1536]{1,0:T(8,128)(2,1)} fusion(f32[1764,768]{1,0:T(8,128)} %reshape.266, f32[1764]{0:T(1024)S(1)} %rsqrt.31, f32[1764]{0:T(1024)S(1)} %div.31, bf16[768,2304]{1,0:T(8,128)(2,1)} %param.12), kind=kOutput, calls=%fused_computation.20 | convolution fusion | flops 4168571904 | bytes 13223712 | tf_op jit(solution)/shard_map/dot_general | solution.py:113
  99.9 9.2 %reshape_reshape.6 = bf16[3,14,3,14,1536]{4,3,2,1,0:T(8,128)(2,1)} reshape(bf16[1764,1536]{1,0:T(8,128)(2,1)} %convolution_convert_fusion) | data formatting | bytes 10838016 | tf_op jit(solution)/shard_map/reshape;reshape | solution.py:43
  109.1 6.3 %copy.117 = bf16[3,14,3,14,1536]{4,3,1,2,0:T(8,128)(2,1)} copy(bf16[3,14,3,14,1536]{4,3,2,1,0:T(8,128)(2,1)} %reshape_reshape.6) | data formatting | bytes 10838016 | tf_op jit(solution)/shard_map/reshape;reshape | solution.py:43
  115.4 8.5 %reshape.256 = bf16[9,196,1536]{2,1,0:T(8,128)(2,1)} reshape(bf16[3,3,14,14,1536]{4,3,2,1,0:T(8,128)(2,1)} %bitcast.53) | data formatting | bytes 10838016 | tf_op jit(solution)/shard_map/reshape | solution.py:44
  123.9 5.4 %fusion.63 = (bf16[9,196,768]{2,1,0:T(8,128)(2,1)}, bf16[9,196,768]{2,1,0:T(8,128)(2,1)}) fusion(bf16[9,196,1536]{2,1,0:T(8,128)(2,1)} %reshape.256), kind=kLoop, calls=%fused_computation.110 | loop fusion | bytes 10838016 | tf_op jit(solution)/shard_map/slice | solution.py:61
  129.3 5.4 %copy.90 = bf16[9,196,768]{1,2,0:T(8,128)(2,1)} copy(bf16[9,196,768]{2,1,0:T(8,128)(2,1)} %get-tuple-element.4) | data formatting | bytes 5419008 | tf_op jit(solution)/shard_map/slice | solution.py:61
  134.7 5.4 %copy.88 = bf16[9,196,768]{1,2,0:T(8,128)(2,1)} copy(bf16[9,196,768]{2,1,0:T(8,128)(2,1)} %get-tuple-element.5) | data formatting | bytes 5419008 | tf_op jit(solution)/shard_map/slice | solution.py:62
  140.1 14.6 %fusion.14 = f32[9,12,196,196]{2,3,1,0:T(8,128)} fusion(bf16[9,196,12,64]{1,3,2,0:T(8,128)(2,1)} %bitcast.55, bf16[9,196,12,64]{3,2,1,0:T(8,128)(2,1)} %reshape_reshape.7), kind=kOutput, calls=%fused_computation.24 | convolution fusion | flops 531062784 | bytes 22014720 | tf_op jit(solution)/shard_map/nqhd,nkhd->nhqk/dot_general | solution.py:63
  154.7 28.6 %fusion.67 = (f32[9,12,196]{2,1,0:T(8,128)S(1)}, f32[9,12,196,196]{2,3,1,0:T(8,128)}) fusion(f32[9,12,196,196]{2,3,1,0:T(8,128)} %fusion.14, pred[9,196]{1,0:T(8,128)(4,1)S(1)} %broadcast_in_dim.35), kind=kOutput, calls=%fused_computation.114 | output fusion | flops 24893764 | bytes 33277860 | tf_op jit(solution)/shard_map/sub | solution.py:68
  183.3 12.5 %convert_bitcast_fusion = bf16[9,196,12,64]{1,3,2,0:T(8,128)(2,1)} fusion(bf16[9,196,12,64]{1,3,2,0:T(8,128)(2,1)} %bitcast.58, f32[9,12,196,196]{2,3,1,0:T(8,128)} %get-tuple-element.15, f32[9,12,196]{2,1,0:T(8,128)S(1)} %get-tuple-element.14), kind=kOutput, calls=%fused_computation.29 | convolution fusion | flops 540715392 | bytes 22099392 | tf_op jit(solution)/shard_map/nhqk,nkhd->nqhd/dot_general | solution.py:70
  195.7 10.6 %copy.93 = bf16[9,196,12,64]{3,2,1,0:T(8,128)(2,1)} copy(bf16[9,196,12,64]{1,3,2,0:T(8,128)(2,1)} %convert_bitcast_fusion) | data formatting | bytes 5419008 | tf_op jit(solution)/shard_map/convert_element_type | solution.py:71
  206.3 10.1 %convert_element_type.120 = bf16[3,3,14,14,768]{4,3,2,1,0:T(8,128)(2,1)} reshape(bf16[9,196,12,64]{3,2,1,0:T(8,128)(2,1)} %copy.93) | data formatting | bytes 5419008 | tf_op jit(solution)/shard_map/convert_element_type | solution.py:71
  216.4 3.7 copy.94
  220.1 5.4 %reshape.261 = bf16[42,42,768]{2,1,0:T(8,128)(2,1)} reshape(bf16[3,14,3,14,768]{4,3,2,1,0:T(8,128)(2,1)} %copy.94) | data formatting | bytes 5419008 | tf_op jit(solution)/shard_map/reshape | solution.py:52
  225.5 2.0 slice.60
  228.8 3.6 fusion.68
  234.0 13.1 %add_convert_fusion = bf16[784,768]{1,0:T(8,128)(2,1)S(1)} fusion(f32[784,768]{1,0:T(8,128)} %copy-done.5, bf16[3072,768]{1,0:T(8,128)(2,1)} %param.15, bf16[768,3072]{1,0:T(8,128)(2,1)} %param.14, f32[784]{0:T(1024)S(1)} %add_rsqrt_fusion.2, f32[784]{0:T(1024)S(1)} %broadcast_multiply_fusion.2), kind=kOutput, calls=%fused_computation.36 | convolution fusion | flops 7423438848 | bytes 13056128 | tf_op jit(solution)/shard_map/dot_general | solution.py:82
  247.1 2.2 reshape.268
  249.4 4.2 reduce_sum.102
  253.5 1.9 multiply_convert_fusion.10
  256.8 11.9 %gather_fusion = bf16[3136,4,192]{2,1,0:T(4,128)(2,1)} fusion(bf16[4,196,192]{2,0,1:T(4,128)(2,1)S(1)} %bitcast.51, s32[4096]{0:T(1024)S(1)} %pad_clamp_fusion), kind=kCustom, calls=%fused_computation | custom fusion | bytes 9646336 | tf_op jit(solution)/shard_map/jit(_take)/gather | solution.py:169
  268.8 6.3 %copy.101 = bf16[4,3136,192]{2,1,0:T(8,128)(2,1)} copy(bf16[4,3136,192]{2,0,1:T(4,128)(2,1)} %bitcast.52) | data formatting | bytes 9633792 | tf_op jit(solution)/shard_map/jit(_take)/gather | solution.py:169
  275.1 10.6 %gather.11 = bf16[128,2,49,192]{3,2,1,0:T(8,128)(2,1)} reshape(bf16[4,3136,192]{2,1,0:T(8,128)(2,1)} %copy.101) | data formatting | bytes 9633792 | tf_op jit(solution)/shard_map/jit(_take)/gather | solution.py:169
  285.7 6.5 %broadcast_select_fusion = bf16[128,2,49,192]{3,2,1,0:T(8,128)(2,1)S(1)} fusion(bf16[128,2,49,192]{3,2,1,0:T(8,128)(2,1)} %gather.11, pred[128,2,49]{2,1,0:T(4,128)(4,1)S(1)} %bitcast.59), kind=kLoop, calls=%fused_computation.21 | loop fusion | flops 2408448 | bytes 9646336 | tf_op jit(solution)/shard_map/jit(_take)/select_n | solution.py:169
  292.3 4.6 copy.102
  296.9 31.5 %all-to-all-start = ((bf16[128,2,49,192]{3,1,2,0:T(2,128)(2,1)}), bf16[128,2,49,192]{3,1,2,0:T(2,128)(2,1)}, u32[]{:S(2)}, u32[]{:S(2)}) async-start(bf16[128,2,49,192]{3,1,2,0:T(2,128)(2,1)} %copy.102), calls=%async_computation | async-start | bytes 12845056 | tf_op jit(solution)/shard_map/all_to_all | solution.py:172
  329.9 76.3 %all-to-all-done = bf16[128,2,49,192]{3,1,2,0:T(2,128)(2,1)} async-done(((bf16[128,2,49,192]{3,1,2,0:T(2,128)(2,1)}), bf16[128,2,49,192]{3,1,2,0:T(2,128)(2,1)}, u32[]{:S(2)}, u32[]{:S(2)}) %all-to-all-start) | async-done | bytes 4816928 | tf_op jit(solution)/shard_map/all_to_all | solution.py:172
  406.2 7.1 %copy.103 = bf16[128,2,49,192]{3,2,1,0:T(8,128)(2,1)} copy(bf16[128,2,49,192]{3,1,2,0:T(2,128)(2,1)} %all-to-all-done) | data formatting | bytes 9633792 | tf_op jit(solution)/shard_map/all_to_all | solution.py:172
  413.3 5.7 %gather_fusion.1 = bf16[128,49,192]{2,1,0:T(8,128)(2,1)} fusion(bf16[256,49,192]{2,1,0:T(8,128)(2,1)} %bitcast.54, s32[1024]{0:T(1024)S(1)} %pad_clamp_fusion.1), kind=kCustom, calls=%fused_computation.1 | custom fusion | bytes 4817408 | tf_op jit(solution)/shard_map/jit(_take)/gather | solution.py:179
  418.9 4.2 broadcast_select_fusion.1
  423.1 14.6 %fusion.35 = bf16[128,1024]{1,0:T(8,128)(2,1)} fusion(bf16[49,192,1024]{1,2,0:T(8,128)(2,1)} %all-gather.2.cloned.1.call-done, bf16[128,49,192]{2,1,0:T(8,128)(2,1)} %broadcast_select_fusion.1), kind=kOutput, calls=%fused_computation.51 | convolution fusion | flops 2466381824 | bytes 21938176 | tf_op jit(solution)/shard_map/dot_general | solution.py:180
  438.6 19.1 %reduce-scatter.3.cloned.1.call-done = bf16[128,256]{1,0:T(8,128)(2,1)} async-done(((bf16[128,1024]{1,0:T(8,128)(2,1)}), bf16[128,256]{1,0:T(8,128)(2,1)}) %reduce-scatter.3.cloned.1.call-update) | async-done | bytes 65552 | tf_op jit(solution)/shard_map/reduce_scatter | solution.py:187
  461.4 19.1 %reduce-scatter.5.cloned.1.call-done = bf16[128,256]{1,0:T(8,128)(2,1)} async-done(((bf16[128,1024]{1,0:T(8,128)(2,1)}), bf16[128,256]{1,0:T(8,128)(2,1)}) %reduce-scatter.5.cloned.1.call-update) | async-done | bytes 65552 | tf_op jit(solution)/shard_map/reduce_scatter | solution.py:194
  (77 shorter events, 30.0 us)
Async XLA Ops:
  7.2 450.5 %copy-start = (bf16[1024,1024]{1,0:T(8,128)(2,1)S(1)}, bf16[1024,1024]{1,0:T(8,128)(2,1)}, u32[]{:S(2)}) copy-start(bf16[1024,1024]{1,0:T(8,128)(2,1)} %param.18) | copy-start | bytes 6291460
  7.2 11.3 %copy-start.1 = (bf16[28,28,768]{2,1,0:T(8,128)(2,1)S(1)}, bf16[28,28,768]{2,1,0:T(8,128)(2,1)}, u32[]{:S(2)}) copy-start(bf16[28,28,768]{2,1,0:T(8,128)(2,1)} %param.11) | copy-start | bytes 3612676
  7.2 415.9 %all-gather.2.cloned.1.call-start = ((), (), s32[]{:S(2)}) async-start(), calls=%async_computation.3 | async-start | bytes 26492928 | tf_op jit(solution)/shard_map/all_gather | solution.py:182
  9.9 48.7 %collective-permute-start = (bf16[7,28,768]{2,1,0:T(8,128)(2,1)}, bf16[7,28,768]{2,1,0:T(8,128)(2,1)}, u32[]{:S(2)}, u32[]{:S(2)}) collective-permute-start(bf16[7,28,768]{2,1,0:T(8,128)(2,1)} %get-tuple-element.9), channel_id=1, source_target_pairs={{0,32},{32,64},{64,96},{1,33},{33,65},{65,97},{2,34},{34,66},{66,9... | collective-permute-start | bytes 903176 | tf_op jit(solution)/shard_map/ppermute | solution.py:23
  14.2 45.6 %collective-permute-start.1 = (bf16[7,28,768]{2,1,0:T(8,128)(2,1)}, bf16[7,28,768]{2,1,0:T(8,128)(2,1)}, u32[]{:S(2)}, u32[]{:S(2)}) collective-permute-start(bf16[7,28,768]{2,1,0:T(8,128)(2,1)} %get-tuple-element.8), channel_id=1, source_target_pairs={{32,0},{64,32},{96,64},{33,1},{65,33},{97,65},{34,2},{66,34},{98,6... | collective-permute-start | bytes 903176 | tf_op jit(solution)/shard_map/ppermute | solution.py:25
  58.7 7.6 %copy-start.6 = (s32[3136,1]{0,1:T(1,128)S(1)}, s32[3136,1]{0,1:T(1,128)}, u32[]{:S(2)}) copy-start(s32[3136,1]{0,1:T(1,128)} %add.238) | copy-start | bytes 37636
  60.8 1.3 copy-start.2
  63.2 3.2 collective-permute-start.2
  64.8 5.6 %collective-permute-start.3 = (bf16[42,7,768]{2,1,0:T(8,128)(2,1)}, bf16[42,7,768]{2,1,0:T(8,128)(2,1)S(1)}, u32[]{:S(2)}, u32[]{:S(2)}) collective-permute-start(bf16[42,7,768]{2,1,0:T(8,128)(2,1)} %get-tuple-element.7), channel_id=1, source_target_pairs={{1,0},{2,1},{3,2},{4,3},{5,4},{6,5},{7,6},{8,7},{9,8},{10,9},{11,1... | collective-permute-start | bytes 1354760 | tf_op jit(solution)/shard_map/ppermute | solution.py:25
  232.5 1.5 copy-start.5
  247.1 6.4 %copy-start.3 = (bf16[784,768]{1,0:T(8,128)(2,1)}, bf16[784,768]{1,0:T(8,128)(2,1)S(1)}, u32[]{:S(2)}) copy-start(bf16[784,768]{1,0:T(8,128)(2,1)S(1)} %add_convert_fusion) | copy-start | bytes 3612676
  296.9 109.3 %all-to-all-start = ((bf16[128,2,49,192]{3,1,2,0:T(2,128)(2,1)}), bf16[128,2,49,192]{3,1,2,0:T(2,128)(2,1)}, u32[]{:S(2)}, u32[]{:S(2)}) async-start(bf16[128,2,49,192]{3,1,2,0:T(2,128)(2,1)} %copy.102), calls=%async_computation | async-start | bytes 12845056 | tf_op jit(solution)/shard_map/all_to_all | solution.py:172
  328.4 129.3 %reduce-scatter.3.cloned.1.call-start = ((), (), s32[]{:S(2)}) async-start(), calls=%async_computation.4 | async-start | bytes 327680 | tf_op jit(solution)/shard_map/reduce_scatter | solution.py:187
  423.1 37.1 %copy-start.4 = (bf16[784,768]{1,0:T(8,128)(2,1)S(1)}, bf16[784,768]{1,0:T(8,128)(2,1)}, u32[]{:S(2)}) copy-start(bf16[784,768]{1,0:T(8,128)(2,1)} %copy-done.3) | copy-start | bytes 3612676
  437.8 42.7 %reduce-scatter.5.cloned.1.call-start = ((), (), s32[]{:S(2)}) async-start(), calls=%async_computation.5 | async-start | bytes 327680 | tf_op jit(solution)/shard_map/reduce_scatter | solution.py:194
Sparse Core Ops, SparseCore 0:
  10.3 100.7 all-gather.1
  437.9 19.7 reduce-scatter.2
  460.1 20.2 reduce-scatter.4
where the time goes:
time: 498 us; the launch traced here: 489 us
  local copies, waits for them, and re-layouts  176 us (35%)
  waiting for transfers between devices  119 us (24%)
  matrix products  74.7 us (15%)
  other arithmetic  64.8 us (13%)
  starting transfers between devices  40 us (8%)
  between operations  14.3 us (3%)
    all_to_all x1, waiting for transfers between devices, shards(): lax.all_to_all(outgoing, ('row', 'col'), split_axis=0, concat_axis=0, til...  76.3 us
    all_to_all x1, starting transfers between devices, shards(): lax.all_to_all(outgoing, ('row', 'col'), split_axis=0, concat_axis=0, til...  31.5 us
    gather x3, local copies, waits for them, and re-layouts, shards(): gathered = jnp.take(grouped, sample_at, axis=1)  28.8 us
    sub x1, other arithmetic, attend(): weights = jnp.exp(scores - row_max)  28.6 us
    convert_element_type x2, local copies, waits for them, and re-layouts, attend(): return blended.reshape(window_count, length, width_all).astype(jnp.bfloat16)  20.7 us
    reduce_scatter x1, waiting for transfers between devices, shards(): lax.psum_scatter(second_part.astype(jnp.bfloat16), 'row', scatter_dimensi...  19.1 us
    reduce_scatter x1, waiting for transfers between devices, shards(): lax.psum_scatter(first_sum.astype(jnp.bfloat16), 'row', scatter_dimension...  19.1 us
    another operation x2, local copies, waits for them, and re-layouts, to_windows(): shaped = lattice.reshape(row_blocks, window, col_blocks, window, channels)  15.5 us
  transfers between devices with their start and end apart: 8, of which 5 were waited for; matrix products, arithmetic and copies ran while one was open for 60% of the time, Pallas kernels for 0%

commit v1 on v0

v1 whole, which is shorter than its diff:
```python
import functools

import jax
import jax.numpy as jnp
from jax import lax
from jax.experimental import pallas as pl
from jax.experimental.pallas import tpu as pltpu
from jax.sharding import PartitionSpec as P

ROWS = 4
COLS = 32
D = 768
SIDE = 28
HEADS = 12
MLP = 3072
FC = 1024
S0, S1, S2, OWN = 0, 224, 672, 896
TOP, BOT, LEFT, RIGHT, TL, TR, BL, BR, HALO = 0, 240, 480, 704, 928, 992, 1056, 1120, 1184
HALO_COPIES = (
    (S0 + 160, 64, TOP, 1, 0),
    (S1 + 336, 112, TOP + 64, 1, 0),
    (S2 + 160, 64, TOP + 176, 1, 0),
    (S0, 64, BOT, -1, 0),
    (S1, 112, BOT + 64, -1, 0),
    (S2, 64, BOT + 176, -1, 0),
    (S2, 224, LEFT, 0, 1),
    (S0, 224, RIGHT, 0, -1),
    (S2 + 160, 64, TL, 1, 1),
    (S0 + 160, 64, TR, 1, -1),
    (S2, 64, BL, -1, 1),
    (S0, 64, BR, -1, -1),
)
MESH = pl.DeviceIdType.MESH
F32 = jnp.float32
BF16 = jnp.bfloat16
VMEM_SPEC = pl.BlockSpec(memory_space=pltpu.VMEM)


def greet(peers):
    barrier = pltpu.get_barrier_semaphore()
    for peer in peers:
        pl.semaphore_signal(barrier, inc=1, device_id=peer, device_id_type=MESH)
    pl.semaphore_wait(barrier, len(peers))


def halo_kernel(tokens_ref, own_ref, halo_ref, wide_ref, send_sem, recv_sem):
    row, col = lax.axis_index("row"), lax.axis_index("col")

    def near(dr, dc):
        return lax.rem(row + dr + ROWS, ROWS), lax.rem(col + dc + COLS, COLS)

    barrier = pltpu.get_barrier_semaphore()
    peers = [near(dr, dc) for dr in (-1, 0, 1) for dc in (-1, 0, 1) if (dr, dc) != (0, 0)]
    for peer in peers:
        pl.semaphore_signal(barrier, inc=1, device_id=peer, device_id_type=MESH)
    for y in range(0, SIDE, 2):
        for a in range(2):
            wide_ref[a, 0:SIDE, :] = tokens_ref[y + a].astype(F32)
        own_ref[S0 + y * 8 : S0 + y * 8 + 16, :] = jnp.concatenate(
            [wide_ref[a, 0:8, :] for a in range(2)], axis=0
        ).astype(BF16)
        own_ref[S1 + y * 16 : S1 + y * 16 + 32, :] = jnp.concatenate(
            [wide_ref[a, 7:23, :] for a in range(2)], axis=0
        ).astype(BF16)
        own_ref[S2 + y * 8 : S2 + y * 8 + 16, :] = jnp.concatenate(
            [wide_ref[a, 20:28, :] for a in range(2)], axis=0
        ).astype(BF16)
    pl.semaphore_wait(barrier, len(peers))
    copies = [
        pltpu.make_async_remote_copy(
            src_ref=own_ref.at[pl.ds(src, rows)],
            dst_ref=halo_ref.at[pl.ds(dst, rows)],
            send_sem=send_sem.at[n],
            recv_sem=recv_sem.at[n],
            device_id=near(dr, dc),
            device_id_type=MESH,
        )
        for n, (src, rows, dst, dr, dc) in enumerate(HALO_COPIES)
    ]
    for copy in copies:
        copy.start()
    for copy in copies:
        copy.wait()


def exchange_halo(tokens):
    return pl.pallas_call(
        halo_kernel,
        out_shape=(
            jax.ShapeDtypeStruct((OWN, D), BF16),
            jax.ShapeDtypeStruct((HALO, D), BF16),
        ),
        in_specs=[VMEM_SPEC],
        out_specs=(VMEM_SPEC, VMEM_SPEC),
        scratch_shapes=[
            pltpu.VMEM((2, 32, D), F32),
            pltpu.SemaphoreType.DMA((len(HALO_COPIES),)),
            pltpu.SemaphoreType.DMA((len(HALO_COPIES),)),
        ],
        compiler_params=pltpu.CompilerParams(collective_id=0, has_side_effects=True),
        name="halo",
    )(tokens)


def norm(values):
    center = values - jnp.mean(values, axis=-1, keepdims=True)
    spread = jnp.mean(center * center, axis=-1, keepdims=True)
    return (center * lax.rsqrt(spread + 1e-6)).astype(BF16)


def window_sources():
    strips = {
        "s0": (S0, 8, (TOP, 8), (BOT, 0), False),
        "s1": (S1, 16, (TOP + 64, 0), (BOT + 64, 0), False),
        "s2": (S2, 8, (TOP + 176, 8), (BOT + 176, 0), False),
        "l": (LEFT, 8, (TL, 8), (BL, 0), True),
        "r": (RIGHT, 8, (TR, 8), (BR, 0), True),
    }
    windows = []
    for wy in range(3):
        for names in (("s0", "l"), ("s1",), ("s2", "r")):
            pieces = []
            for name in names:
                base, cells, top, bottom, outer = strips[name]
                if wy == 0:
                    pieces.append((True, top[0], top[1], 7 * cells))
                    pieces.append((outer, base, 0, 7 * cells))
                elif wy == 1:
                    pieces.append((outer, base + 7 * cells, 0, 14 * cells))
                else:
                    pieces.append((outer, base + 21 * cells, 0, 7 * cells))
                    pieces.append((True, bottom[0], bottom[1], 7 * cells))
            windows.append(pieces)
    return windows


QUERY_ROWS = [
    ((S0, 56), (S1, 112), (S2, 56)),
    ((S0 + 56, 112), (S1 + 112, 224), (S2 + 56, 112)),
    ((S0 + 168, 56), (S1 + 336, 112), (S2 + 168, 56)),
]


def block_kernel(
    own_ref,
    halo_ref,
    project_in_ref,
    project_out_ref,
    expand_ref,
    reduce_ref,
    features_ref,
    pooled_ref,
    window_ref,
    kv_ref,
    query_ref,
    mixed_ref,
    wide_ref,
    small_ref,
):
    row, col = lax.axis_index("row"), lax.axis_index("col")
    for w, pieces in enumerate(window_sources()):
        place = w * 224
        for outer, base, skip, rows in pieces:
            source = halo_ref if outer else own_ref
            start = base + skip
            low = start // 16 * 16
            high = -(-(start + rows) // 16) * 16
            values = source[low:high, :].astype(F32)
            window_ref[place : place + rows, :] = values[start - low : start - low + rows]
            place += rows

    def project(w, carry):
        at = pl.ds(pl.multiple_of(w * 224, 224), 224)
        normed = norm(window_ref[at, :])
        kv_ref[w, 0:224, :] = jnp.dot(
            normed, project_in_ref[:, D:], preferred_element_type=F32
        ).astype(BF16)
        kv_ref[w, 224:256, :] = jnp.zeros((32, 2 * D), BF16)
        return carry

    lax.fori_loop(0, 9, project, 0)

    def ask(n, carry):
        at = pl.ds(pl.multiple_of(n * 224, 224), 224)
        normed = norm(own_ref[at, :].astype(F32))
        query_ref[at, :] = (
            jnp.dot(normed, project_in_ref[:, :D], preferred_element_type=F32)
            .astype(BF16)
            .astype(F32)
            * 0.125
        )
        return carry

    lax.fori_loop(0, 4, ask, 0)

    lane = lax.broadcasted_iota(jnp.int32, (1, 256), 1)
    left_half = lax.broadcasted_iota(jnp.int32, (1, 128), 1) < 64
    for wy in range(3):
        for wx in range(3):
            w = wy * 3 + wx
            start, rows = QUERY_ROWS[wy][wx]
            eighth = lax.rem(lane, 8)
            if wx == 0:
                keep = ((lane < 112) & (eighth != 7)) | ((lane >= 112) & (eighth != 0))
                keep = keep & ((lane < 112) | (col > 0))
            elif wx == 1:
                keep = lax.rem(lane, 16) < 14
            else:
                keep = ((lane < 112) & (eighth != 0)) | ((lane >= 112) & (eighth != 7))
                keep = keep & ((lane < 112) | (col < COLS - 1))
            keep = keep & (lane < 224)
            half = lax.rem(lane, 112) < 56 if wx != 1 else lane < 112
            if wy == 0:
                keep = keep & (jnp.logical_not(half) | (row > 0))
            elif wy == 2:
                keep = keep & (half | (row < ROWS - 1))
            bias = jnp.where(keep, 0.0, -1e30).astype(F32)

            def pair(h, carry, w=w, start=start, rows=rows, bias=bias):
                first = pl.multiple_of(h * 128, 128)
                asked = query_ref[start : start + rows, pl.ds(first, 128)]
                both = jnp.concatenate(
                    [jnp.where(left_half, asked, 0.0), jnp.where(left_half, 0.0, asked)],
                    axis=0,
                ).astype(BF16)
                keys = kv_ref[w, :, pl.ds(first, 128)]
                values = kv_ref[w, :, pl.ds(pl.multiple_of(D + h * 128, 128), 128)]
                scores = (
                    lax.dot_general(
                        both, keys, (((1,), (1,)), ((), ())), preferred_element_type=F32
                    )
                    + bias
                )
                weights = jnp.exp(scores - jnp.max(scores, axis=-1, keepdims=True))
                total = jnp.sum(weights, axis=-1, keepdims=True)
                mixed = jnp.dot(weights.astype(BF16), values, preferred_element_type=F32) / total
                mixed_ref[start : start + rows, pl.ds(first, 128)] = jnp.where(
                    left_half, mixed[:rows], mixed[rows:]
                )
                return carry

            lax.fori_loop(0, HEADS // 2, pair, 0)

    def finish(n, carry):
        at = pl.ds(pl.multiple_of(n * 224, 224), 224)
        after = own_ref[at, :].astype(F32) + jnp.dot(
            mixed_ref[at, :].astype(BF16), project_out_ref[...], preferred_element_type=F32
        )
        normed = norm(after)
        total = after
        for part in range(MLP // D):
            units = slice(part * D, (part + 1) * D)
            hidden = jax.nn.gelu(
                jnp.dot(normed, expand_ref[:, units], preferred_element_type=F32)
            ).astype(BF16)
            total = total + jnp.dot(hidden, reduce_ref[units, :], preferred_element_type=F32)
        mixed_ref[at, :] = total.astype(BF16).astype(F32)
        return carry

    lax.fori_loop(0, 4, finish, 0)

    wide_ref[:, :, SIDE:, :] = jnp.zeros((6, SIDE, 32 - SIDE, 128), F32)

    def place_row(y, carry):
        for n in range(6):
            lanes = slice(n * 128, (n + 1) * 128)
            wide_ref[n, y, 0:8, :] = mixed_ref[pl.ds(pl.multiple_of(S0 + y * 8, 8), 8), lanes]
            wide_ref[n, y, 20:28, :] = mixed_ref[pl.ds(pl.multiple_of(S2 + y * 8, 8), 8), lanes]
            middle = mixed_ref[pl.ds(pl.multiple_of(S1 + y * 16, 16), 16), lanes]
            wide_ref[n, y, 7:21, :] = middle[:14]
        features_ref[y] = jnp.concatenate(
            [wide_ref[n, y, 0:SIDE, :] for n in range(6)], axis=1
        ).astype(BF16)
        return carry

    lax.fori_loop(0, SIDE, place_row, 0)

    def pool(u, carry):
        for n in range(6):
            total = (
                wide_ref[n, 2 * u, pl.ds(0, 16, stride=2), :]
                + wide_ref[n, 2 * u, pl.ds(1, 16, stride=2), :]
                + wide_ref[n, 2 * u + 1, pl.ds(0, 16, stride=2), :]
                + wide_ref[n, 2 * u + 1, pl.ds(1, 16, stride=2), :]
            )
            small_ref[pl.ds(pl.multiple_of(u * 16, 16), 16), n * 128 : (n + 1) * 128] = (
                total * 0.25
            )
        return carry

    lax.fori_loop(0, SIDE // 2, pool, 0)
    small_ref[224:256, :] = jnp.zeros((32, D), F32)
    for group, first in enumerate((0, 128, 384, 512)):
        values = small_ref[:, first : first + 256]
        if group % 2:
            values = pltpu.roll(values, 192, 1)
        pooled_ref[group] = values.astype(BF16)


def block(own, halo, project_in, project_out, expand_weight, reduce_weight):
    return pl.pallas_call(
        block_kernel,
        out_shape=(
            jax.ShapeDtypeStruct((SIDE, SIDE, D), BF16),
            jax.ShapeDtypeStruct((ROWS, 256, 256), BF16),
        ),
        in_specs=[VMEM_SPEC] * 6,
        out_specs=(VMEM_SPEC, VMEM_SPEC),
        scratch_shapes=[
            pltpu.VMEM((9 * 224, D), F32),
            pltpu.VMEM((9, 256, 2 * D), BF16),
            pltpu.VMEM((OWN, D), F32),
            pltpu.VMEM((OWN, D), F32),
            pltpu.VMEM((6, SIDE, 32, 128), F32),
            pltpu.VMEM((256, D), F32),
        ],
        compiler_params=pltpu.CompilerParams(vmem_limit_bytes=60 * 1024 * 1024),
        cost_estimate=pl.CostEstimate(
            flops=18_000_000_000, bytes_accessed=22_000_000, transcendentals=6_000_000
        ),
        name="block",
    )(own, halo, project_in, project_out, expand_weight, reduce_weight)


def swap_kernel(pooled_ref, out_ref, send_sem, recv_sem, own_sem):
    row, col = lax.axis_index("row"), lax.axis_index("col")
    base = col // 2 * 2
    me = row * 2 + col % 2
    others = [(me + n) % 8 for n in range(1, 8)]
    greet([(other // 2, base + other % 2) for other in others])
    own = pltpu.make_async_copy(pooled_ref.at[row], out_ref.at[me], own_sem)
    own.start()
    copies = [
        pltpu.make_async_remote_copy(
            src_ref=pooled_ref.at[other // 2],
            dst_ref=out_ref.at[me],
            send_sem=send_sem.at[n],
            recv_sem=recv_sem.at[n],
            device_id=(other // 2, base + other % 2),
            device_id_type=MESH,
        )
        for n, other in enumerate(others)
    ]
    for copy in copies:
        copy.start()
    own.wait()
    for copy in copies:
        copy.wait()


def swap_groups(pooled):
    return pl.pallas_call(
        swap_kernel,
        out_shape=jax.ShapeDtypeStruct((8, 256, 256), BF16),
        in_specs=[VMEM_SPEC],
        out_specs=VMEM_SPEC,
        scratch_shapes=[
            pltpu.SemaphoreType.DMA((7,)),
            pltpu.SemaphoreType.DMA((7,)),
            pltpu.SemaphoreType.DMA,
        ],
        compiler_params=pltpu.CompilerParams(collective_id=1, has_side_effects=True),
        name="swap",
    )(pooled)


def first_kernel(pooled_ref, tile_ref, code_ref, weight_ref, out_ref, code_at, crops, total):
    step = pl.program_id(0)
    col = lax.axis_index("col")

    @pl.when(step == 0)
    def _():
        lane = lax.broadcasted_iota(jnp.int32, (COLS, 128), 1)
        for t in range(8):
            tile = t // 2 * COLS + col // 2 * 2 + t % 2
            here = tile_ref[...] == tile
            first = jnp.min(jnp.where(here, lane, 127), axis=1, keepdims=True)
            last = jnp.max(jnp.where(here, lane, 0), axis=1, keepdims=True)
            for rank, pick in enumerate((first, last)):
                code = jnp.sum(jnp.where(lane == pick, code_ref[...], 0), axis=1, keepdims=True)
                code_at[t, rank * COLS : (rank + 1) * COLS, :] = jnp.broadcast_to(
                    code, (COLS, 128)
                )
        total[...] = jnp.zeros_like(total)

    spot = lax.broadcasted_iota(jnp.int32, (64, 128), 1)
    for t in range(8):
        code = code_at[t]
        down = 1 + lax.rem(code // 2, 2)
        right = 1 + lax.rem(code, 2)
        position = code // 4 + step * 16 * down
        picks = []
        for j in range(7):
            low = (position == spot).astype(F32)
            high = (position == spot + 128).astype(F32)
            picks.append(jnp.concatenate([low, high], axis=1).astype(BF16))
            position = position + right
        found = jnp.dot(
            jnp.concatenate(picks, axis=0), pooled_ref[t], preferred_element_type=F32
        ).astype(BF16)
        for j in range(7):
            crops[j, t * 64 : (t + 1) * 64, :] = found[j * 64 : (j + 1) * 64, :192]
    summed = total[...]
    for j in range(7):
        summed = summed + lax.dot_general(
            crops[j], weight_ref[j], (((1,), (1,)), ((), ())), preferred_element_type=F32
        )
    total[...] = summed

    @pl.when(step == 6)
    def _():
        to = lax.broadcasted_iota(jnp.int32, (512, 512), 0)
        source = lax.rem(to // 2, 8) * 64 + lax.rem(to, 2) * 32 + to // 16
        order = (source == lax.broadcasted_iota(jnp.int32, (512, 512), 1)).astype(F32).astype(BF16)
        out_ref[...] = jnp.dot(
            order, summed.astype(BF16), preferred_element_type=F32
        ).astype(BF16)


def first_layer(pooled, tiles, codes, weight):
    return pl.pallas_call(
        first_kernel,
        grid=(7,),
        out_shape=jax.ShapeDtypeStruct((512, 512), BF16),
        in_specs=[
            pl.BlockSpec((8, 256, 256), lambda i: (0, 0, 0)),
            pl.BlockSpec((COLS, 128), lambda i: (0, 0)),
            pl.BlockSpec((COLS, 128), lambda i: (0, 0)),
            pl.BlockSpec((7, 512, 192), lambda i: (i, 0, 0)),
        ],
        out_specs=pl.BlockSpec((512, 512), lambda i: (0, 0)),
        scratch_shapes=[
            pltpu.VMEM((8, 64, 128), jnp.int32),
            pltpu.VMEM((7, 512, 192), BF16),
            pltpu.VMEM((512, 512), F32),
        ],
        compiler_params=pltpu.CompilerParams(vmem_limit_bytes=40 * 1024 * 1024),
        cost_estimate=pl.CostEstimate(
            flops=8_000_000_000, bytes_accessed=12_000_000, transcendentals=0
        ),
        name="first_layer",
    )(pooled, tiles, codes, weight)


def head_kernel(
    sums_ref,
    tile_ref,
    first_bias_ref,
    second_ref,
    second_bias_ref,
    out_ref,
    shares,
    reduced,
    landed,
    parts,
    final,
    second_rows,
    row_send,
    row_recv,
    col_send,
    col_recv,
    last_send,
    last_recv,
    weight_sem,
):
    row, col = lax.axis_index("row"), lax.axis_index("col")
    rows_near = [lax.rem(row + n, ROWS) for n in range(1, ROWS)]
    barrier = pltpu.get_barrier_semaphore()
    for other in rows_near:
        pl.semaphore_signal(barrier, inc=1, device_id=(other, col), device_id_type=MESH)

    def greet_col(n, carry):
        pl.semaphore_signal(
            barrier, inc=1, device_id=(row, lax.rem(col + n, COLS)), device_id_type=MESH
        )
        return carry

    lax.fori_loop(1, COLS, greet_col, 0)
    loads = [
        pltpu.make_async_copy(
            second_ref.at[pl.ds(row * 256 + k * 64 + h * 32, 32)],
            second_rows.at[h, pl.ds(k * 32, 32)],
            weight_sem.at[h * 4 + k],
        )
        for h in range(2)
        for k in range(4)
    ]
    for load in loads:
        load.start()
    pl.semaphore_wait(barrier, ROWS - 1 + COLS - 1)

    copies = [
        pltpu.make_async_remote_copy(
            src_ref=sums_ref.at[:, pl.ds(pl.multiple_of(other * 128, 128), 128)],
            dst_ref=shares.at[n],
            send_sem=row_send.at[n],
            recv_sem=row_recv.at[n],
            device_id=(other, col),
            device_id_type=MESH,
        )
        for n, other in enumerate(rows_near)
    ]
    for copy in copies:
        copy.start()
    for copy in copies:
        copy.wait()
    summed = sums_ref[:, pl.ds(pl.multiple_of(row * 128, 128), 128)].astype(F32)
    for n in range(ROWS - 1):
        summed = summed + shares[n].astype(F32)
    reduced[...] = summed.astype(BF16)

    def to_col(n):
        other = lax.rem(col + n, COLS)
        return pltpu.make_async_remote_copy(
            src_ref=reduced.at[pl.ds(pl.multiple_of(other * 16, 16), 16)],
            dst_ref=landed.at[col],
            send_sem=col_send.at[n],
            recv_sem=col_recv.at[n],
            device_id=(row, other),
            device_id_type=MESH,
        )

    def start_col(n, carry):
        to_col(n).start()
        return carry

    lax.fori_loop(1, COLS, start_col, 0)
    landed[col] = reduced[pl.ds(pl.multiple_of(col * 16, 16), 16), :]

    tiles = tile_ref[pl.ds(col, 1), :]
    down = lax.broadcasted_iota(jnp.int32, (128, 128), 0)
    across = lax.broadcasted_iota(jnp.int32, (128, 128), 1)
    spread = jnp.broadcast_to(tiles, (128, 128))
    mine = jnp.sum(jnp.where(down == across, spread, 0), axis=1, keepdims=True)
    earlier = jnp.where((mine == spread) & (across < down), 1, 0)
    rank = jnp.max(earlier, axis=1, keepdims=True)
    tile_col = lax.rem(mine, COLS)
    slot = tile_col // 2 * 16 + (mine // COLS * 2 + lax.rem(tile_col, 2)) * 2 + rank
    select = (
        (slot == lax.broadcasted_iota(jnp.int32, (128, 256), 1)).astype(F32).astype(BF16)
    )

    def wait_col(n, carry):
        to_col(n).wait()
        return carry

    lax.fori_loop(1, COLS, wait_col, 0)
    for load in loads:
        load.wait()
    second = None
    for h in range(2):
        slots = jnp.concatenate([landed[2 * k + h] for k in range(16)], axis=0)
        chosen = jnp.dot(select, slots, preferred_element_type=F32)
        hidden = jnp.maximum(chosen + first_bias_ref[row, h : h + 1, :], 0.0).astype(BF16)
        part = jnp.dot(hidden, second_rows[h], preferred_element_type=F32)
        second = part if second is None else second + part
    parts[...] = second.astype(BF16)
    copies = [
        pltpu.make_async_remote_copy(
            src_ref=parts.at[:, pl.ds(pl.multiple_of(other * 256, 256), 256)],
            dst_ref=final.at[n],
            send_sem=last_send.at[n],
            recv_sem=last_recv.at[n],
            device_id=(other, col),
            device_id_type=MESH,
        )
        for n, other in enumerate(rows_near)
    ]
    for copy in copies:
        copy.start()
    for copy in copies:
        copy.wait()
    summed = parts[:, pl.ds(pl.multiple_of(row * 256, 256), 256)].astype(F32)
    for n in range(ROWS - 1):
        summed = summed + final[n].astype(F32)
    out_ref[...] = jnp.maximum(summed + second_bias_ref[pl.ds(row, 1), :], 0.0).astype(BF16)


def head(sums, tiles, first_bias, second_weight, second_bias):
    return pl.pallas_call(
        head_kernel,
        out_shape=jax.ShapeDtypeStruct((128, 256), BF16),
        in_specs=[VMEM_SPEC, VMEM_SPEC, VMEM_SPEC, pl.BlockSpec(memory_space=pl.ANY), VMEM_SPEC],
        out_specs=VMEM_SPEC,
        scratch_shapes=[
            pltpu.VMEM((ROWS - 1, 512, 128), BF16),
            pltpu.VMEM((512, 128), BF16),
            pltpu.VMEM((COLS, 16, 128), BF16),
            pltpu.VMEM((128, FC), BF16),
            pltpu.VMEM((ROWS - 1, 128, 256), BF16),
            pltpu.VMEM((2, 128, FC), BF16),
            pltpu.SemaphoreType.DMA((ROWS - 1,)),
            pltpu.SemaphoreType.DMA((ROWS - 1,)),
            pltpu.SemaphoreType.DMA((COLS,)),
            pltpu.SemaphoreType.DMA((COLS,)),
            pltpu.SemaphoreType.DMA((ROWS - 1,)),
            pltpu.SemaphoreType.DMA((ROWS - 1,)),
            pltpu.SemaphoreType.DMA((8,)),
        ],
        compiler_params=pltpu.CompilerParams(collective_id=2, has_side_effects=True),
        name="head",
    )(sums, tiles, first_bias, second_weight, second_bias)


def shards(
    tokens,
    project_in,
    project_out,
    expand_weight,
    reduce_weight,
    first_weight,
    first_bias,
    second_weight,
    second_bias,
    box_tile,
    box_shape,
):
    weight = lax.all_gather(
        first_weight.transpose(0, 2, 1),
        "col",
        axis=1,
        tiled=True,
        axis_index_groups=[list(range(core, COLS, 2)) for core in range(2)],
    )
    own, halo = exchange_halo(tokens)
    features, pooled = block(own, halo, project_in, project_out, expand_weight, reduce_weight)
    tiles = box_tile.reshape(COLS, 128)
    codes = (
        (box_shape[:, 0] * 16 + box_shape[:, 1]) * 4
        + (box_shape[:, 2] - 1) * 2
        + (box_shape[:, 3] - 1)
    ).reshape(COLS, 128)
    sums = first_layer(swap_groups(pooled), tiles, codes, weight)
    bias = first_bias.reshape(ROWS, 4, 2, 32).transpose(0, 2, 1, 3).reshape(ROWS, 2, 128)
    box_features = head(sums, tiles, bias, second_weight, second_bias.reshape(ROWS, 256))
    return (features, box_features)


def solution(mesh):
    return jax.shard_map(
        shards,
        mesh=mesh,
        in_specs=(
            P("row", "col", None),
            P(),
            P(),
            P(),
            P(),
            P(None, "row", "col"),
            P(),
            P(),
            P(),
            P(),
            P(),
        ),
        out_specs=(P("row", "col", None), P("col", "row")),
        check_vma=False,
    )
```

time: 498 us -> 162 us (0.33); the launches traced: 489 us -> 162 us
  local copies, waits for them, and re-layouts: 176 us -> 9.52 us
  Pallas kernels: 0 us -> 135 us
  waiting for transfers between devices: 119 us -> 2.97 us
  matrix products: 74.7 us -> 0 us
  other arithmetic: 64.8 us -> 0.06 us
  starting transfers between devices: 40 us -> 0.04 us
    pallas_call x0 -> x5, Pallas kernels: none -> 135 us  [the longest x1 54.2 us: block(): pl.pallas_call(block_kernel, out_shape=(jax.ShapeDtypeStruct((SIDE, SIDE,...]
    all_to_all x1 -> x0, waiting for transfers between devices: 76.3 us -> none  [shards(): lax.all_to_all(outgoing, ('row', 'col'), split_axis=0, concat_axis=0, til...]
    dot_general x8 -> x0, matrix products: 74.7 us -> none  [the longest x1 14.6 us: shards(): lax.dot_general(own_crops, lax.all_gather(first_weight, 'col', axis=2, ti...]
    reduce_scatter x2 -> x0, waiting for transfers between devices: 38.1 us -> none  [the longest x1 19.1 us: shards(): lax.psum_scatter(second_part.astype(jnp.bfloat16), 'row', scatter_dimensi...]
    gather x4 -> x0, local copies, waits for them, and re-layouts: 34.5 us -> none  [the longest x3 28.8 us: shards(): gathered = jnp.take(grouped, sample_at, axis=1)]
    convert_element_type x6 -> x0, local copies, waits for them, and re-layouts: 34.4 us -> none  [the longest x2 20.7 us: attend(): return blended.reshape(window_count, length, width_all).astype(jnp.bfloat16)]
    all_to_all x1 -> x0, starting transfers between devices: 31.5 us -> none  [shards(): lax.all_to_all(outgoing, ('row', 'col'), split_axis=0, concat_axis=0, til...]
    sub x2 -> x0, other arithmetic: 29.3 us -> none  [the longest x1 28.6 us: attend(): weights = jnp.exp(scores - row_max)]
  transfers between devices with their start and end apart: 8 -> 1, of which waited for: 5 -> 1; matrix products, arithmetic and copies ran while one was open for 60% -> 1% of each run, Pallas kernels for 0% -> 58%
where the time goes in v1:
time: 162 us
  Pallas kernels  135 us (83%)
  between operations  14.1 us (9%)
  local copies, waits for them, and re-layouts  9.52 us (6%)
  waiting for transfers between devices  2.97 us (2%)
    pallas_call x1, Pallas kernels, block(): pl.pallas_call(block_kernel, out_shape=(jax.ShapeDtypeStruct((SIDE, SIDE,...  54.2 us
    pallas_call x1, Pallas kernels, head(): pl.pallas_call(head_kernel, out_shape=jax.ShapeDtypeStruct((128, 256), BF...  26.3 us
    pallas_call x1, Pallas kernels, exchange_halo(): pl.pallas_call(halo_kernel, out_shape=(jax.ShapeDtypeStruct((OWN, D), BF1...  23.4 us
    pallas_call x1, Pallas kernels, swap_groups(): pl.pallas_call(swap_kernel, out_shape=jax.ShapeDtypeStruct((8, 256, 256),...  16.7 us
    pallas_call x1, Pallas kernels, first_layer(): pl.pallas_call(first_kernel, grid=(7,), out_shape=jax.ShapeDtypeStruct((5...  14.2 us
    unnamed x15, local copies, waits for them, and re-layouts  8.15 us
  transfers between devices with their start and end apart: 1, of which 1 were waited for; matrix products, arithmetic and copies ran while one was open for 1% of the time, Pallas kernels for 58%

profile of v1, /device:TPU:0, one launch (start us, length us, event | category | flops | bytes accessed | tf_op | source)
XLA Modules:
  0.0 161.5 jit_solution(12494216991225205389)
XLA Ops:
  7.2 0.0 all-gather.2.cloned.1.call-start
  7.2 0.7 all-gather.2.cloned.1.call-update
  7.9 23.4 %halo.1 = (bf16[896,768]{1,0:T(8,128)(2,1)}, bf16[1184,768]{1,0:T(8,128)(2,1)}) custom-call(bf16[28,28,768]{2,1,0:T(8,128)(2,1)} %tokens_ref.1), custom_call_target="tpu_custom_call" | custom-call | tf_op jit(solution)/shard_map/halo/pallas_call | solution.py:87
  31.4 0.0 copy-start.5
  31.4 0.0 copy-start.6
  31.4 0.0 copy-start.4
  31.4 0.0 copy-start.2
  31.4 54.2 %block.1 = (bf16[28,28,768]{2,1,0:T(8,128)(2,1)}, bf16[4,256,256]{2,1,0:T(8,128)(2,1)}) custom-call(bf16[896,768]{1,0:T(8,128)(2,1)} %get-tuple-element.6.own_ref, bf16[1184,768]{1,0:T(8,128)(2,1)} %get-tuple-element.7.halo_ref, bf16[768,2304]{1,0:T(8,128)(2,1)} %project_in_ref.1, bf16[768,768]{1,0:T(8,128)(2,1)} %project_out_ref.1, ...), custom_call_target="tpu_custom_call" | custom-call | flops 17999998976 | bytes 22000000 | tf_op jit(solution)/shard_map/block/pallas_call | solution.py:301
  85.6 16.7 %swap.1.pooled_ref = bf16[8,256,256]{2,1,0:T(8,128)(2,1)} custom-call(bf16[4,256,256]{2,1,0:T(8,128)(2,1)} %get-tuple-element.9.pooled_ref), custom_call_target="tpu_custom_call" | custom-call | tf_op jit(solution)/shard_map/swap/pallas_call | solution.py:352
  102.3 0.0 copy-done.5
  102.3 0.1 reshape.34
  102.4 0.7 reshape.35.first_bias_ref
  103.1 0.0 copy-done.6
  103.1 0.6 reshape.36.second_bias_ref
  103.7 0.0 copy-done.4
  103.7 0.1 add_add_fusion
  103.7 2.3 %all-gather.2.cloned.1.call-done.weight_ref = bf16[49,512,192]{2,1,0:T(8,128)(2,1)} async-done(((bf16[49,32,192]{2,1,0:T(8,128)(2,1)}), bf16[49,512,192]{2,1,0:T(8,128)(2,1)}) %all-gather.2.cloned.1.call-update) | async-done | bytes 9633808 | tf_op jit(solution)/shard_map/all_gather | solution.py:618
  106.0 0.0 copy-done.2
  106.0 0.0 copy-start
  106.0 1.2 copy-done
  107.3 0.0 copy-start.3
  107.3 4.6 %copy-done.3 = bf16[49,512,192]{2,1,0:T(8,128)(2,1)S(1)} copy-done((bf16[49,512,192]{2,1,0:T(8,128)(2,1)S(1)}, bf16[49,512,192]{2,1,0:T(8,128)(2,1)}, u32[]{:S(2)}) %copy-start.3) | copy-done | bytes 9633816
  111.9 14.2 %first_layer.1.sums_ref = bf16[512,512]{1,0:T(8,128)(2,1)S(1)} custom-call(bf16[8,256,256]{2,1,0:T(8,128)(2,1)S(1)} %copy-done, s32[32,128]{1,0:T(8,128)S(1)} %bitcast.5, s32[32,128]{1,0:T(8,128)S(1)} %bitcast.6, bf16[49,512,192]{2,1,0:T(8,128)(2,1)S(1)} %copy-done.3), custom_call_target="tpu_custom_call" | custom-call | flops 8000000000 | bytes 12000000 | tf_op jit(solution)/shard_map/first_layer/pallas_call | solution.py:421
  126.1 0.0 copy-start.1
  126.1 0.8 copy-done.1
  126.9 26.3 %head.1 = bf16[128,256]{1,0:T(8,128)(2,1)} custom-call(bf16[512,512]{1,0:T(8,128)(2,1)} %copy-done.1, s32[32,128]{1,0:T(8,128)} %bitcast.4, f32[4,2,128]{2,1,0:T(2,128)} %reshape.35.first_bias_ref, bf16[1024,1024]{1,0:T(8,128)(2,1)} %second_ref.1, f32[4,256]{1,0:T(4,128)} %reshape.36.second_bias_ref), custom_call_target="tpu_custom_call" | custom-call | tf_op jit(solution)/shard_map/head/pallas_call | solution.py:580
  153.2 1.5 copy.15
  (1 shorter events, 0.0 us)
Async XLA Ops:
  7.2 98.9 %all-gather.2.cloned.1.call-start = ((), (), s32[]{:S(2)}) async-start(), calls=%async_computation | async-start | bytes 13647872 | tf_op jit(solution)/shard_map/all_gather | solution.py:618
  31.4 70.9 %copy-start.5 = (f32[1024]{0:T(1024)S(1)}, f32[1024]{0:T(1024)}, u32[]{:S(2)}) copy-start(f32[1024]{0:T(1024)} %param.17) | copy-start | bytes 12292
  31.4 71.7 %copy-start.6 = (f32[1024]{0:T(1024)S(1)}, f32[1024]{0:T(1024)}, u32[]{:S(2)}) copy-start(f32[1024]{0:T(1024)} %param.19) | copy-start | bytes 12292
  31.4 72.3 %copy-start.4 = (s32[4096,4]{0,1:T(4,128)S(1)}, s32[4096,4]{0,1:T(4,128)}, u32[]{:S(2)}) copy-start(s32[4096,4]{0,1:T(4,128)} %param.21) | copy-start | bytes 196612
  31.4 74.6 %copy-start.2 = (s32[4096,1]{0,1:T(1,128)S(1)}, s32[4096,1]{0,1:T(1,128)}, u32[]{:S(2)}) copy-start(s32[4096,1]{0,1:T(1,128)} %param.20) | copy-start | bytes 49156
  106.0 1.2 copy-start
  107.3 4.7 %copy-start.3 = (bf16[49,512,192]{2,1,0:T(8,128)(2,1)S(1)}, bf16[49,512,192]{2,1,0:T(8,128)(2,1)}, u32[]{:S(2)}) copy-start(bf16[49,512,192]{2,1,0:T(8,128)(2,1)} %all-gather.2.cloned.1.call-done.weight_ref) | copy-start | bytes 28901380
  126.1 0.8 copy-start.1
Sparse Core Ops, SparseCore 0:
  10.1 95.8 all-gather.1

commit v2 on v1

v2 whole, which is shorter than its diff:
```python
import jax
import jax.numpy as jnp
from jax import lax
from jax.experimental import pallas as pl
from jax.experimental.pallas import tpu as pltpu
from jax.sharding import PartitionSpec as P

ROWS = 4
COLS = 32
D = 768
SIDE = 28
HEADS = 12
MLP = 3072
FC = 1024
S0, S1, S2, OWN = 0, 224, 672, 896
TOP, BOT, LEFT, RIGHT, TL, TR, BL, BR, HALO = 0, 256, 512, 736, 960, 1024, 1088, 1152, 1216
HALO_COPIES = (
    (S0 + 160, 64, TOP, 1, 0),
    (S1 + 320, 128, TOP + 64, 1, 0),
    (S2 + 160, 64, TOP + 192, 1, 0),
    (S0, 64, BOT, -1, 0),
    (S1, 128, BOT + 64, -1, 0),
    (S2, 64, BOT + 192, -1, 0),
    (S2, 224, LEFT, 0, 1),
    (S0, 224, RIGHT, 0, -1),
    (S2 + 160, 64, TL, 1, 1),
    (S0 + 160, 64, TR, 1, -1),
    (S2, 64, BL, -1, 1),
    (S0, 64, BR, -1, -1),
)
UNITS = 32
BIN_PARTS = ((0, 13), (13, 12), (25, 12), (37, 12))
GATHER = 28
MESH = pl.DeviceIdType.MESH
F32 = jnp.float32
BF16 = jnp.bfloat16
VMEM_SPEC = pl.BlockSpec(memory_space=pltpu.VMEM)


def norm(values):
    center = values - jnp.mean(values, axis=-1, keepdims=True)
    spread = jnp.mean(center * center, axis=-1, keepdims=True)
    return (center * lax.rsqrt(spread + 1e-6)).astype(BF16)


def window_keys(wy, wx):
    strips = (
        ((False, S0, 8, TOP, BOT), (True, LEFT, 8, TL, BL)),
        ((False, S1, 16, TOP + 64, BOT + 64),),
        ((False, S2, 8, TOP + 192, BOT + 192), (True, RIGHT, 8, TR, BR)),
    )[wx]
    pieces = []
    for outer, base, cells, top, bottom in strips:
        if wy == 0:
            pieces += [(outer, base, 8 * cells), (True, top, 8 * cells)]
        elif wy == 1:
            pieces += [(outer, base + 6 * cells, 16 * cells)]
        else:
            pieces += [(outer, base + 20 * cells, 8 * cells), (True, bottom, 8 * cells)]
    return pieces


def window_bias(wy, wx, row, col):
    lane = lax.broadcasted_iota(jnp.int32, (1, 256), 1)
    cells = 16 if wx == 1 else 8
    line = lax.rem(lane // cells, 16)
    cell = lax.rem(lane, cells)
    if wx == 1:
        keep = cell < 14
    else:
        own_spare, outer_spare = (7, 0) if wx == 0 else (0, 7)
        there = col > 0 if wx == 0 else col < COLS - 1
        keep = ((lane < 128) & (cell != own_spare)) | (
            (lane >= 128) & (cell != outer_spare) & there
        )
    if wy == 0:
        keep = keep & ((line < 7) | ((line > 8) & (row > 0)))
    elif wy == 1:
        keep = keep & (line > 0) & (line < 15)
    else:
        keep = keep & (((line > 0) & (line < 8)) | ((line >= 8) & (line < 15) & (row < ROWS - 1)))
    return jnp.where(keep, 0.0, -1e30).astype(F32)


QUERY_ROWS = [
    ((S0, 56), (S1, 112), (S2, 56)),
    ((S0 + 56, 112), (S1 + 112, 224), (S2 + 56, 112)),
    ((S0 + 168, 56), (S1 + 336, 112), (S2 + 168, 56)),
]


def gather_stages(row, col, part_ref, whole_ref, send_sem, recv_sem):
    z, y, core = col // 8, lax.rem(col // 2, 4), lax.rem(col, 2)
    mine = z * 4 + y
    numbers = iter(range(GATHER))

    def send(to, bins, chunk, width=1, own=False):
        n = next(numbers)
        rows = pl.ds(pl.multiple_of(chunk * UNITS, UNITS), UNITS * width)
        here = whole_ref.at[pl.ds(*bins), rows]
        return pltpu.make_async_remote_copy(
            src_ref=part_ref.at[pl.ds(*bins)] if own else here,
            dst_ref=here,
            send_sem=send_sem.at[n],
            recv_sem=recv_sem.at[n],
            device_id=(row, to),
            device_id_type=MESH,
        )

    def near(dz, dy):
        return lax.rem(z + dz + 4, 4), lax.rem(y + dy + 4, 4)

    def device(dz, dy):
        nz, ny = near(dz, dy)
        return nz * 8 + ny * 2 + core

    first = (0, 25), (25, 24)
    up = [device(0, 1), device(1, 0)]
    down = [device(0, -1), device(-1, 0)]
    steps = ((0, 1), (1, 0))
    stages = [[], [], [], []]
    for axis in range(2):
        for to in (up[axis], down[axis]):
            stages[0].append(send(to, first[axis], mine, own=True))
    for axis in range(2):
        dz, dy = steps[axis]
        for sign, to, part in ((-1, up[axis], 0), (1, down[axis], 1)):
            nz, ny = near(sign * dz, sign * dy)
            stages[1].append(send(to, BIN_PARTS[2 * axis + part], nz * 4 + ny))
    for to in (up[1], down[1]):
        stages[2].append(send(to, first[0], z * 4, 4))
    for to in (up[0], down[0]):
        for n in range(4):
            stages[2].append(send(to, first[1], n * 4 + y))
    for sign, to, part in ((-1, up[1], 0), (1, down[1], 1)):
        stages[3].append(send(to, BIN_PARTS[part], near(sign, 0)[0] * 4, 4))
    for sign, to, part in ((-1, up[0], 2), (1, down[0], 3)):
        for n in range(4):
            stages[3].append(send(to, BIN_PARTS[part], n * 4 + near(0, sign)[1]))
    return stages, [(row, to) for to in up + down], mine


def block_kernel(
    tokens_ref,
    project_in_hbm,
    project_out_hbm,
    expand_hbm,
    reduce_hbm,
    part_ref,
    features_ref,
    pooled_ref,
    whole_ref,
    own_ref,
    halo_ref,
    project_in_ref,
    project_out_ref,
    expand_ref,
    reduce_ref,
    kv_own_ref,
    kv_halo_ref,
    query_ref,
    mixed_ref,
    wide_ref,
    small_ref,
    load_sem,
    send_sem,
    recv_sem,
    gather_send,
    gather_recv,
):
    row, col = lax.axis_index("row"), lax.axis_index("col")
    stages, gather_peers, mine = gather_stages(
        row, col, part_ref, whole_ref, gather_send, gather_recv
    )

    def near(dr, dc):
        return lax.rem(row + dr + ROWS, ROWS), lax.rem(col + dc + COLS, COLS)

    peers = [near(dr, dc) for dr in (-1, 0, 1) for dc in (-1, 0, 1) if (dr, dc) != (0, 0)]
    peers = peers + gather_peers
    barrier = pltpu.get_barrier_semaphore()
    for peer in peers:
        pl.semaphore_signal(barrier, inc=1, device_id=peer, device_id_type=MESH)
    loads = [
        pltpu.make_async_copy(source, target, load_sem.at[n])
        for n, (source, target) in enumerate(
            (
                (project_in_hbm, project_in_ref),
                (project_out_hbm, project_out_ref),
                (expand_hbm, expand_ref),
                (reduce_hbm, reduce_ref),
                (part_ref, whole_ref.at[:, pl.ds(pl.multiple_of(mine * UNITS, UNITS), UNITS)]),
            )
        )
    ]
    for load in loads:
        load.start()
    for y in range(0, SIDE, 2):
        for a in range(2):
            wide_ref[0:6, a, 0:SIDE, :] = jnp.stack(
                [
                    tokens_ref[y + a, :, n * 128 : (n + 1) * 128].astype(F32)
                    for n in range(6)
                ]
            )
        for base, cells, x in ((S0, 8, 0), (S1, 16, 7), (S2, 8, 20)):
            own_ref[base + y * cells : base + (y + 2) * cells, :] = jnp.concatenate(
                [
                    jnp.concatenate(
                        [wide_ref[n, a, x : x + cells, :] for n in range(6)], axis=1
                    )
                    for a in range(2)
                ],
                axis=0,
            ).astype(BF16)
    pl.semaphore_wait(barrier, len(peers))
    halo_copies = [
        pltpu.make_async_remote_copy(
            src_ref=own_ref.at[pl.ds(src, rows)],
            dst_ref=halo_ref.at[pl.ds(dst, rows)],
            send_sem=send_sem.at[n],
            recv_sem=recv_sem.at[n],
            device_id=near(dr, dc),
            device_id_type=MESH,
        )
        for n, (src, rows, dst, dr, dc) in enumerate(HALO_COPIES)
    ]
    for copy in halo_copies:
        copy.start()
    for copy in stages[0]:
        copy.start()

    loads[0].wait()

    def project_own(n, carry):
        at = pl.ds(pl.multiple_of(n * 224, 224), 224)
        normed = norm(own_ref[at, :].astype(F32))
        query_ref[at, :] = (
            jnp.dot(normed, project_in_ref[:, :D], preferred_element_type=F32)
            .astype(BF16)
            .astype(F32)
            * 0.125
        )
        kv_own_ref[at, :] = jnp.dot(
            normed, project_in_ref[:, D:], preferred_element_type=F32
        ).astype(BF16)
        return carry

    lax.fori_loop(0, 4, project_own, 0)
    for copy in halo_copies:
        copy.wait()
    for copy in stages[0]:
        copy.wait_recv()
    for copy in stages[1]:
        copy.start()

    def project_halo(n, carry):
        at = pl.ds(pl.multiple_of(n * 304, 304), 304)
        normed = norm(halo_ref[at, :].astype(F32))
        kv_halo_ref[at, :] = jnp.dot(
            normed, project_in_ref[:, D:], preferred_element_type=F32
        ).astype(BF16)
        return carry

    lax.fori_loop(0, 4, project_halo, 0)
    loads[4].wait()
    for copy in stages[1]:
        copy.wait_recv()
    for copy in stages[2]:
        copy.start()

    left_half = lax.broadcasted_iota(jnp.int32, (1, 128), 1) < 64
    ones = jnp.ones((256, 128), BF16)
    for wy in range(3):
        for wx in range(3):
            start, rows = QUERY_ROWS[wy][wx]
            bias = window_bias(wy, wx, row, col)
            pieces = window_keys(wy, wx)
            for h in range(HEADS // 2):
                lanes = slice(h * 128, (h + 1) * 128)
                asked = query_ref[start : start + rows, lanes]
                both = jnp.concatenate(
                    [jnp.where(left_half, asked, 0.0), jnp.where(left_half, 0.0, asked)],
                    axis=0,
                ).astype(BF16)

                def read(first, pieces=pieces):
                    return jnp.concatenate(
                        [
                            (kv_halo_ref if outer else kv_own_ref)[
                                base : base + count, first : first + 128
                            ]
                            for outer, base, count in pieces
                        ],
                        axis=0,
                    )

                scores = (
                    lax.dot_general(
                        both,
                        read(h * 128),
                        (((1,), (1,)), ((), ())),
                        preferred_element_type=F32,
                    )
                    + bias
                )
                weights = jnp.exp(scores - jnp.max(scores, axis=-1, keepdims=True)).astype(BF16)
                values = jnp.concatenate([read(D + h * 128), ones], axis=1)
                mixed = jnp.dot(weights, values, preferred_element_type=F32)
                mixed = mixed[:, :128] / mixed[:, 128:]
                mixed_ref[start : start + rows, lanes] = jnp.where(
                    left_half, mixed[:rows], mixed[rows:]
                )

    for load in loads[1:4]:
        load.wait()
    for copy in stages[2]:
        copy.wait_recv()
    for copy in stages[3]:
        copy.start()

    def finish(n, carry):
        at = pl.ds(pl.multiple_of(n * 224, 224), 224)
        after = own_ref[at, :].astype(F32) + jnp.dot(
            mixed_ref[at, :].astype(BF16), project_out_ref[...], preferred_element_type=F32
        )
        normed = norm(after)
        total = after
        for part in range(MLP // D):
            units = slice(part * D, (part + 1) * D)
            hidden = jax.nn.gelu(
                jnp.dot(normed, expand_ref[:, units], preferred_element_type=F32)
            ).astype(BF16)
            total = total + jnp.dot(hidden, reduce_ref[units, :], preferred_element_type=F32)
        mixed_ref[at, :] = total.astype(BF16).astype(F32)
        return carry

    lax.fori_loop(0, 4, finish, 0)

    wide_ref[:, :, SIDE:, :] = jnp.zeros((6, SIDE, 32 - SIDE, 128), F32)

    def place_row(y, carry):
        for n in range(6):
            lanes = slice(n * 128, (n + 1) * 128)
            wide_ref[n, y, 0:8, :] = mixed_ref[pl.ds(pl.multiple_of(S0 + y * 8, 8), 8), lanes]
            wide_ref[n, y, 20:28, :] = mixed_ref[pl.ds(pl.multiple_of(S2 + y * 8, 8), 8), lanes]
            middle = mixed_ref[pl.ds(pl.multiple_of(S1 + y * 16, 16), 16), lanes]
            wide_ref[n, y, 7:21, :] = middle[:14]
        features_ref[y] = jnp.concatenate(
            [wide_ref[n, y, 0:SIDE, :] for n in range(6)], axis=1
        ).astype(BF16)
        return carry

    lax.fori_loop(0, SIDE, place_row, 0)

    def pool(u, carry):
        for n in range(6):
            total = (
                wide_ref[n, 2 * u, pl.ds(0, 16, stride=2), :]
                + wide_ref[n, 2 * u, pl.ds(1, 16, stride=2), :]
                + wide_ref[n, 2 * u + 1, pl.ds(0, 16, stride=2), :]
                + wide_ref[n, 2 * u + 1, pl.ds(1, 16, stride=2), :]
            )
            small_ref[pl.ds(pl.multiple_of(u * 16, 16), 16), n * 128 : (n + 1) * 128] = (
                total * 0.25
            )
        return carry

    lax.fori_loop(0, SIDE // 2, pool, 0)
    small_ref[224:256, :] = jnp.zeros((32, D), F32)
    for group, first in enumerate((0, 128, 384, 512)):
        values = small_ref[:, first : first + 256]
        if group % 2:
            values = pltpu.roll(values, 192, 1)
        pooled_ref[group] = values.astype(BF16)


    for copy in stages[3]:
        copy.wait_recv()
    for stage in stages:
        for copy in stage:
            copy.wait_send()


def block(tokens, project_in, project_out, expand_weight, reduce_weight, first_weight):
    bins, units, depth = first_weight.shape
    return pl.pallas_call(
        block_kernel,
        out_shape=(
            jax.ShapeDtypeStruct((SIDE, SIDE, D), BF16),
            jax.ShapeDtypeStruct((ROWS, 256, 256), BF16),
            jax.ShapeDtypeStruct((bins, units * COLS // 2, depth), BF16),
        ),
        in_specs=[VMEM_SPEC] + [pl.BlockSpec(memory_space=pl.ANY)] * 5,
        out_specs=(VMEM_SPEC, VMEM_SPEC, pl.BlockSpec(memory_space=pl.ANY)),
        scratch_shapes=[
            pltpu.VMEM((OWN, D), BF16),
            pltpu.VMEM((HALO, D), BF16),
            pltpu.VMEM((D, 3 * D), BF16),
            pltpu.VMEM((D, D), BF16),
            pltpu.VMEM((D, MLP), BF16),
            pltpu.VMEM((MLP, D), BF16),
            pltpu.VMEM((OWN, 2 * D), BF16),
            pltpu.VMEM((HALO, 2 * D), BF16),
            pltpu.VMEM((OWN, D), F32),
            pltpu.VMEM((OWN, D), F32),
            pltpu.VMEM((6, SIDE, 32, 128), F32),
            pltpu.VMEM((256, D), F32),
            pltpu.SemaphoreType.DMA((5,)),
            pltpu.SemaphoreType.DMA((len(HALO_COPIES),)),
            pltpu.SemaphoreType.DMA((len(HALO_COPIES),)),
            pltpu.SemaphoreType.DMA((GATHER,)),
            pltpu.SemaphoreType.DMA((GATHER,)),
        ],
        compiler_params=pltpu.CompilerParams(
            collective_id=0, has_side_effects=True, vmem_limit_bytes=60 * 1024 * 1024
        ),
        cost_estimate=pl.CostEstimate(
            flops=18_000_000_000, bytes_accessed=22_000_000, transcendentals=6_000_000
        ),
        name="block",
    )(tokens, project_in, project_out, expand_weight, reduce_weight, first_weight)


def boxes_kernel(
    pooled_ref,
    tile_ref,
    code_ref,
    weight_hbm,
    first_bias_ref,
    second_hbm,
    second_bias_ref,
    out_ref,
    group_ref,
    weight_ref,
    code_at,
    crops,
    total,
    sums_ref,
    shares,
    reduced,
    landed,
    parts,
    final,
    second_rows,
    own_sem,
    weight_sem,
    second_sem,
    swap_send,
    swap_recv,
    row_send,
    row_recv,
    col_send,
    col_recv,
    last_send,
    last_recv,
):
    row, col = lax.axis_index("row"), lax.axis_index("col")
    base, core = col // 2 * 2, lax.rem(col, 2)
    rows_near = [lax.rem(row + n, ROWS) for n in range(1, ROWS)]
    barrier = pltpu.get_barrier_semaphore()
    for other in rows_near:
        for side in range(2):
            pl.semaphore_signal(
                barrier, inc=1, device_id=(other, base + side), device_id_type=MESH
            )

    def greet_col(n, carry):
        pl.semaphore_signal(
            barrier, inc=1, device_id=(row, lax.rem(col + n, COLS)), device_id_type=MESH
        )
        return carry

    lax.fori_loop(1, COLS, greet_col, 0)
    me = row * 2 + core
    own = pltpu.make_async_copy(pooled_ref.at[row], group_ref.at[me], own_sem)
    own.start()
    weight_loads = [
        pltpu.make_async_copy(
            weight_hbm.at[pl.ds(i * 7, 7)], weight_ref.at[pl.ds(i * 7, 7)], weight_sem.at[i]
        )
        for i in range(7)
    ]
    for load in weight_loads:
        load.start()
    second_loads = [
        pltpu.make_async_copy(
            second_hbm.at[pl.ds(row * 256 + k * 64 + h * 32, 32)],
            second_rows.at[h, pl.ds(k * 32, 32)],
            second_sem.at[h * 4 + k],
        )
        for h in range(2)
        for k in range(4)
    ]
    for load in second_loads:
        load.start()
    pl.semaphore_wait(barrier, 2 * (ROWS - 1) + COLS - 1)

    others = [lax.rem(me + n, 8) for n in range(1, 8)]
    swaps = [
        pltpu.make_async_remote_copy(
            src_ref=pooled_ref.at[other // 2],
            dst_ref=group_ref.at[me],
            send_sem=swap_send.at[n],
            recv_sem=swap_recv.at[n],
            device_id=(other // 2, base + lax.rem(other, 2)),
            device_id_type=MESH,
        )
        for n, other in enumerate(others)
    ]
    for copy in swaps:
        copy.start()

    lane = lax.broadcasted_iota(jnp.int32, (COLS, 128), 1)
    for t in range(8):
        here = tile_ref[...] == t // 2 * COLS + base + t % 2
        first = jnp.min(jnp.where(here, lane, 127), axis=1, keepdims=True)
        last = jnp.max(jnp.where(here, lane, 0), axis=1, keepdims=True)
        for rank, pick in enumerate((first, last)):
            code = jnp.sum(jnp.where(lane == pick, code_ref[...], 0), axis=1, keepdims=True)
            code_at[t, rank * COLS : (rank + 1) * COLS, :] = jnp.broadcast_to(code, (COLS, 128))
    total[...] = jnp.zeros_like(total)

    tiles = tile_ref[pl.ds(col, 1), :]
    down = lax.broadcasted_iota(jnp.int32, (128, 128), 0)
    across = lax.broadcasted_iota(jnp.int32, (128, 128), 1)
    spread = jnp.broadcast_to(tiles, (128, 128))
    mine = jnp.sum(jnp.where(down == across, spread, 0), axis=1, keepdims=True)
    earlier = jnp.where((mine == spread) & (across < down), 1, 0)
    rank = jnp.max(earlier, axis=1, keepdims=True)
    tile_col = lax.rem(mine, COLS)
    slot = tile_col // 2 * 16 + (mine // COLS * 2 + lax.rem(tile_col, 2)) * 2 + rank
    select = (
        (slot == lax.broadcasted_iota(jnp.int32, (128, 256), 1)).astype(F32).astype(BF16)
    )
    to = lax.broadcasted_iota(jnp.int32, (512, 512), 0)
    source = lax.rem(to // 2, 8) * 64 + lax.rem(to, 2) * 32 + to // 16
    order = (source == lax.broadcasted_iota(jnp.int32, (512, 512), 1)).astype(F32).astype(BF16)

    own.wait()
    for copy in swaps:
        copy.wait()
    spot = lax.broadcasted_iota(jnp.int32, (64, 128), 1)

    def bin_row(i, carry):
        load = pltpu.make_async_copy(
            weight_hbm.at[pl.ds(i * 7, 7)], weight_ref.at[pl.ds(i * 7, 7)], weight_sem.at[i]
        )
        for t in range(8):
            code = code_at[t]
            below = 1 + lax.rem(code // 2, 2)
            right = 1 + lax.rem(code, 2)
            position = code // 4 + i * 16 * below
            picks = []
            for j in range(7):
                low = (position == spot).astype(F32)
                high = (position == spot + 128).astype(F32)
                picks.append(jnp.concatenate([low, high], axis=1).astype(BF16))
                position = position + right
            found = jnp.dot(
                jnp.concatenate(picks, axis=0), group_ref[t], preferred_element_type=F32
            ).astype(BF16)
            for j in range(7):
                crops[j, t * 64 : (t + 1) * 64, :] = found[j * 64 : (j + 1) * 64, :192]
        load.wait()
        summed = total[...]
        for j in range(7):
            summed = summed + lax.dot_general(
                crops[j],
                weight_ref[i * 7 + j],
                (((1,), (1,)), ((), ())),
                preferred_element_type=F32,
            )
        total[...] = summed
        return carry

    lax.fori_loop(0, 7, bin_row, 0)
    sums_ref[...] = jnp.dot(
        order, total[...].astype(BF16), preferred_element_type=F32
    ).astype(BF16)

    copies = [
        pltpu.make_async_remote_copy(
            src_ref=sums_ref.at[:, pl.ds(pl.multiple_of(other * 128, 128), 128)],
            dst_ref=shares.at[n],
            send_sem=row_send.at[n],
            recv_sem=row_recv.at[n],
            device_id=(other, col),
            device_id_type=MESH,
        )
        for n, other in enumerate(rows_near)
    ]
    for copy in copies:
        copy.start()
    for copy in copies:
        copy.wait()
    summed = sums_ref[:, pl.ds(pl.multiple_of(row * 128, 128), 128)].astype(F32)
    for n in range(ROWS - 1):
        summed = summed + shares[n].astype(F32)
    reduced[...] = summed.astype(BF16)

    def to_col(n):
        other = lax.rem(col + n, COLS)
        return pltpu.make_async_remote_copy(
            src_ref=reduced.at[pl.ds(pl.multiple_of(other * 16, 16), 16)],
            dst_ref=landed.at[col],
            send_sem=col_send.at[n],
            recv_sem=col_recv.at[n],
            device_id=(row, other),
            device_id_type=MESH,
        )

    def start_col(n, carry):
        to_col(n).start()
        return carry

    lax.fori_loop(1, COLS, start_col, 0)
    landed[col] = reduced[pl.ds(pl.multiple_of(col * 16, 16), 16), :]

    def wait_col(n, carry):
        to_col(n).wait()
        return carry

    lax.fori_loop(1, COLS, wait_col, 0)
    for load in second_loads:
        load.wait()
    second = None
    for h in range(2):
        slots = jnp.concatenate([landed[2 * k + h] for k in range(16)], axis=0)
        chosen = jnp.dot(select, slots, preferred_element_type=F32)
        hidden = jnp.maximum(chosen + first_bias_ref[row, h : h + 1, :], 0.0).astype(BF16)
        part = jnp.dot(hidden, second_rows[h], preferred_element_type=F32)
        second = part if second is None else second + part
    parts[...] = second.astype(BF16)
    copies = [
        pltpu.make_async_remote_copy(
            src_ref=parts.at[:, pl.ds(pl.multiple_of(other * 256, 256), 256)],
            dst_ref=final.at[n],
            send_sem=last_send.at[n],
            recv_sem=last_recv.at[n],
            device_id=(other, col),
            device_id_type=MESH,
        )
        for n, other in enumerate(rows_near)
    ]
    for copy in copies:
        copy.start()
    for copy in copies:
        copy.wait()
    summed = parts[:, pl.ds(pl.multiple_of(row * 256, 256), 256)].astype(F32)
    for n in range(ROWS - 1):
        summed = summed + final[n].astype(F32)
    out_ref[...] = jnp.maximum(summed + second_bias_ref[pl.ds(row, 1), :], 0.0).astype(BF16)


def boxes(pooled, tiles, codes, weight, first_bias, second_weight, second_bias):
    bins, units, depth = weight.shape
    dma = pltpu.SemaphoreType.DMA
    return pl.pallas_call(
        boxes_kernel,
        out_shape=jax.ShapeDtypeStruct((128, 256), BF16),
        in_specs=[
            VMEM_SPEC,
            VMEM_SPEC,
            VMEM_SPEC,
            pl.BlockSpec(memory_space=pl.ANY),
            VMEM_SPEC,
            pl.BlockSpec(memory_space=pl.ANY),
            VMEM_SPEC,
        ],
        out_specs=VMEM_SPEC,
        scratch_shapes=[
            pltpu.VMEM((8, 256, 256), BF16),
            pltpu.VMEM((bins, units, depth), BF16),
            pltpu.VMEM((8, 64, 128), jnp.int32),
            pltpu.VMEM((7, units, depth), BF16),
            pltpu.VMEM((512, units), F32),
            pltpu.VMEM((512, units), BF16),
            pltpu.VMEM((ROWS - 1, 512, 128), BF16),
            pltpu.VMEM((512, 128), BF16),
            pltpu.VMEM((COLS, 16, 128), BF16),
            pltpu.VMEM((128, FC), BF16),
            pltpu.VMEM((ROWS - 1, 128, 256), BF16),
            pltpu.VMEM((2, 128, FC), BF16),
            dma,
            dma((7,)),
            dma((8,)),
            dma((7,)),
            dma((7,)),
            dma((ROWS - 1,)),
            dma((ROWS - 1,)),
            dma((COLS,)),
            dma((COLS,)),
            dma((ROWS - 1,)),
            dma((ROWS - 1,)),
        ],
        compiler_params=pltpu.CompilerParams(
            collective_id=1, has_side_effects=True, vmem_limit_bytes=56 * 1024 * 1024
        ),
        cost_estimate=pl.CostEstimate(
            flops=9_000_000_000, bytes_accessed=12_000_000, transcendentals=0
        ),
        name="boxes",
    )(pooled, tiles, codes, weight, first_bias, second_weight, second_bias)


def shards(
    tokens,
    project_in,
    project_out,
    expand_weight,
    reduce_weight,
    first_weight,
    first_bias,
    second_weight,
    second_bias,
    box_tile,
    box_shape,
):
    features, pooled, weight = block(
        tokens,
        project_in,
        project_out,
        expand_weight,
        reduce_weight,
        first_weight.transpose(0, 2, 1),
    )
    tiles = box_tile.reshape(COLS, 128)
    codes = (
        (box_shape[:, 0] * 16 + box_shape[:, 1]) * 4
        + (box_shape[:, 2] - 1) * 2
        + (box_shape[:, 3] - 1)
    ).reshape(COLS, 128)
    bias = first_bias.reshape(ROWS, 4, 2, 32).transpose(0, 2, 1, 3).reshape(ROWS, 2, 128)
    box_features = boxes(
        pooled, tiles, codes, weight, bias, second_weight, second_bias.reshape(ROWS, 256)
    )
    return (features, box_features)


def solution(mesh):
    return jax.shard_map(
        shards,
        mesh=mesh,
        in_specs=(
            P("row", "col", None),
            P(),
            P(),
            P(),
            P(),
            P(None, "row", "col"),
            P(),
            P(),
            P(),
            P(),
            P(),
        ),
        out_specs=(P("row", "col", None), P("col", "row")),
        check_vma=False,
    )
```

time: 162 us -> 151 us (0.932)
  between operations: 14.1 us -> 0.71 us
  Pallas kernels: 135 us -> 145 us
  local copies, waits for them, and re-layouts: 9.52 us -> 3.09 us
  waiting for transfers between devices: 2.97 us -> 0 us
    pallas_call x1, Pallas kernels: 54.2 us -> 92.9 us  [block(): pl.pallas_call(block_kernel, out_shape=(jax.ShapeDtypeStruct((SIDE, SIDE,...]
    pallas_call x4 -> x1, Pallas kernels: 80.6 us -> 52.5 us  [boxes(): pl.pallas_call(boxes_kernel, out_shape=jax.ShapeDtypeStruct((128, 256), B...]
    unnamed x15 -> x12, local copies, waits for them, and re-layouts: 8.15 us -> 1.73 us
    all_gather x1 -> x0, waiting for transfers between devices: 2.29 us -> none  [shards(): lax.all_gather(first_weight.transpose(0, 2, 1), 'col', axis=1, tiled=True...]
  transfers between devices with their start and end apart: 1 -> 0, of which waited for: 1 -> 0; matrix products, arithmetic and copies ran while one was open for 1% -> 0% of each run, Pallas kernels for 58% -> 0%
where the time goes in v2:
time: 151 us; the launch traced here: 150 us
  Pallas kernels  145 us (96%)
  local copies, waits for them, and re-layouts  3.09 us (2%)
    pallas_call x1, Pallas kernels, block(): pl.pallas_call(block_kernel, out_shape=(jax.ShapeDtypeStruct((SIDE, SIDE,...  92.9 us
    pallas_call x1, Pallas kernels, boxes(): pl.pallas_call(boxes_kernel, out_shape=jax.ShapeDtypeStruct((128, 256), B...  52.5 us

profile of v2, /device:TPU:0, one launch (start us, length us, event | category | flops | bytes accessed | tf_op | source)
XLA Modules:
  0.0 149.8 jit_solution(13911582766273300268)
XLA Ops:
  0.6 0.0 copy-start.3
  0.6 0.0 copy-start.1
  0.7 0.0 copy-start.4
  0.7 92.9 %block.1 = (bf16[28,28,768]{2,1,0:T(8,128)(2,1)}, bf16[4,256,256]{2,1,0:T(8,128)(2,1)}, bf16[49,512,192]{2,1,0:T(8,128)(2,1)}) custom-call(bf16[28,28,768]{2,1,0:T(8,128)(2,1)} %tokens_ref.1, bf16[768,2304]{1,0:T(8,128)(2,1)} %project_in_hbm.1, bf16[768,768]{1,0:T(8,128)(2,1)} %project_out_hbm.1, bf16[768,3072]{1,0:T(8,128)(2,1)} %expand_hbm.1, ...), custom_call_target="tpu_custom_call" | custom-call | flops 17999998976 | bytes 22000000 | tf_op jit(solution)/shard_map/block/pallas_call | solution.py:387
  93.6 0.0 copy-done.3
  93.6 0.1 reshape.34
  93.7 0.7 reshape.35.first_bias_ref
  94.4 0.0 copy-done.1
  94.4 0.7 add_add_fusion
  95.0 0.0 copy-done.4
  95.0 0.6 reshape.36.second_bias_ref
  95.6 0.0 copy-start
  95.6 52.5 %boxes.1 = bf16[128,256]{1,0:T(8,128)(2,1)} custom-call(bf16[4,256,256]{2,1,0:T(8,128)(2,1)} %get-tuple-element.6.pooled_ref, s32[32,128]{1,0:T(8,128)} %bitcast.7, s32[32,128]{1,0:T(8,128)} %bitcast.5, bf16[49,512,192]{2,1,0:T(8,128)(2,1)} %get-tuple-element.7.weight_hbm, f32[4,2,128]{2,1,0:T(2,128)} %reshape.35.first_bias_ref, ...), custom_call_target="tpu_custom_call" | custom-call | flops 8999999488 | bytes 12000000 | tf_op jit(solution)/shard_map/boxes/pallas_call | solution.py:659
  148.1 0.0 copy-start.2
  148.1 0.0 copy-done
  148.1 1.1 copy.16
  149.2 0.0 copy-done.2
  149.2 0.6 copy.17
  (1 shorter events, 0.0 us)
Async XLA Ops:
  0.6 92.9 %copy-start.3 = (f32[1024]{0:T(1024)S(1)}, f32[1024]{0:T(1024)}, u32[]{:S(2)}) copy-start(f32[1024]{0:T(1024)} %param.17) | copy-start | bytes 12292
  0.6 93.7 %copy-start.1 = (s32[4096,4]{0,1:T(4,128)S(1)}, s32[4096,4]{0,1:T(4,128)}, u32[]{:S(2)}) copy-start(s32[4096,4]{0,1:T(4,128)} %param.21) | copy-start | bytes 196612
  0.7 94.4 %copy-start.4 = (f32[1024]{0:T(1024)S(1)}, f32[1024]{0:T(1024)}, u32[]{:S(2)}) copy-start(f32[1024]{0:T(1024)} %param.19) | copy-start | bytes 12292
  95.6 52.5 %copy-start = (bf16[28,28,768]{2,1,0:T(8,128)(2,1)S(1)}, bf16[28,28,768]{2,1,0:T(8,128)(2,1)}, u32[]{:S(2)}) copy-start(bf16[28,28,768]{2,1,0:T(8,128)(2,1)} %get-tuple-element.10) | copy-start | bytes 3612676
  148.1 1.1 copy-start.2

commit v3 on v2

v3 whole, which is shorter than its diff:
```python
import jax
import jax.numpy as jnp
from jax import lax
from jax.experimental import pallas as pl
from jax.experimental.pallas import tpu as pltpu
from jax.sharding import PartitionSpec as P

ROWS = 4
COLS = 32
D = 768
SIDE = 28
HEADS = 12
MLP = 3072
FC = 1024
S0, S1, S2, OWN = 0, 224, 672, 896
TOP, BOT, LEFT, RIGHT, TL, TR, BL, BR, HALO = 0, 256, 512, 736, 960, 1024, 1088, 1152, 1216
HALO_COPIES = (
    (S0 + 160, 64, TOP, 1, 0),
    (S1 + 320, 128, TOP + 64, 1, 0),
    (S2 + 160, 64, TOP + 192, 1, 0),
    (S0, 64, BOT, -1, 0),
    (S1, 128, BOT + 64, -1, 0),
    (S2, 64, BOT + 192, -1, 0),
    (S2, 224, LEFT, 0, 1),
    (S0, 224, RIGHT, 0, -1),
    (S2 + 160, 64, TL, 1, 1),
    (S0 + 160, 64, TR, 1, -1),
    (S2, 64, BL, -1, 1),
    (S0, 64, BR, -1, -1),
)
QUADS = 12
TILES = 6 * QUADS + 2
HALVES = ((0, 36), (36, 38))
QUARTERS = ((0, 18), (18, 18), (36, 18), (54, 20))
GATHER = 25
UNITS = 32
MESH = pl.DeviceIdType.MESH
F32 = jnp.float32
BF16 = jnp.bfloat16
VMEM_SPEC = pl.BlockSpec(memory_space=pltpu.VMEM)


def norm(values):
    center = values - jnp.mean(values, axis=-1, keepdims=True)
    spread = jnp.mean(center * center, axis=-1, keepdims=True)
    return (center * lax.rsqrt(spread + 1e-6)).astype(BF16)


def window_keys(wy, wx):
    strips = (
        ((False, S0, 8, TOP, BOT), (True, LEFT, 8, TL, BL)),
        ((False, S1, 16, TOP + 64, BOT + 64),),
        ((False, S2, 8, TOP + 192, BOT + 192), (True, RIGHT, 8, TR, BR)),
    )[wx]
    pieces = []
    for outer, base, cells, top, bottom in strips:
        if wy == 0:
            pieces += [(outer, base, 8 * cells), (True, top, 8 * cells)]
        elif wy == 1:
            pieces += [(outer, base + 6 * cells, 16 * cells)]
        else:
            pieces += [(outer, base + 20 * cells, 8 * cells), (True, bottom, 8 * cells)]
    return pieces


def window_bias(wy, wx, row, col):
    lane = lax.broadcasted_iota(jnp.int32, (1, 256), 1)
    cells = 16 if wx == 1 else 8
    line = lax.rem(lane // cells, 16)
    cell = lax.rem(lane, cells)
    if wx == 1:
        keep = cell < 14
    else:
        own_spare, outer_spare = (7, 0) if wx == 0 else (0, 7)
        there = col > 0 if wx == 0 else col < COLS - 1
        keep = ((lane < 128) & (cell != own_spare)) | (
            (lane >= 128) & (cell != outer_spare) & there
        )
    if wy == 0:
        keep = keep & ((line < 7) | ((line > 8) & (row > 0)))
    elif wy == 1:
        keep = keep & (line > 0) & (line < 15)
    else:
        keep = keep & (((line > 0) & (line < 8)) | ((line >= 8) & (line < 15) & (row < ROWS - 1)))
    return jnp.where(keep, 0.0, -1e30).astype(F32)


QUERY_ROWS = [
    ((S0, 56), (S1, 112), (S2, 56)),
    ((S0 + 56, 112), (S1 + 112, 224), (S2 + 56, 112)),
    ((S0 + 168, 56), (S1 + 336, 112), (S2 + 168, 56)),
]


def gather_stages(row, col, whole_ref, send_sem, recv_sem):
    z, y, core = col // 8, lax.rem(col // 2, 4), lax.rem(col, 2)
    numbers = iter(range(GATHER))

    def send(to, place):
        n = next(numbers)
        return pltpu.make_async_remote_copy(
            src_ref=whole_ref.at[place],
            dst_ref=whole_ref.at[place],
            send_sem=send_sem.at[n],
            recv_sem=recv_sem.at[n],
            device_id=(row, to),
            device_id_type=MESH,
        )

    def device(dz, dy):
        return lax.rem(z + dz + 4, 4) * 8 + lax.rem(y + dy + 4, 4) * 2 + core

    def step(at, by):
        return lax.rem(at + by + 4, 4)

    up = [device(0, 1), device(1, 0)]
    down = [device(0, -1), device(-1, 0)]
    stages = [[], [], [], []]
    for axis in range(2):
        for to in (up[axis], down[axis]):
            stages[0].append(send(to, (z, y, pl.ds(*HALVES[axis]))))
    for axis in range(2):
        for sign, to, part in ((-1, up[axis], 0), (1, down[axis], 1)):
            chunk = (z, step(y, sign)) if axis == 0 else (step(z, sign), y)
            stages[1].append(send(to, (*chunk, pl.ds(*QUARTERS[2 * axis + part]))))
    for to in (up[1], down[1]):
        stages[2].append(send(to, (z, slice(None), pl.ds(*HALVES[0]))))
    for to in (up[0], down[0]):
        stages[2].append(send(to, (slice(None), y, pl.ds(*HALVES[1]))))
    for n in range(3):
        for quarter in range(4):
            sign, to = ((-1, up), (1, down))[quarter % 2]
            tiles = pl.ds(QUARTERS[quarter][0] + 6 * n, 6)
            if quarter < 2:
                place = (step(z, sign), slice(None), tiles)
            else:
                place = (slice(None), step(y, sign), tiles)
            stages[3].append(send(to[1 - quarter // 2], place))
    stages[3].append(send(down[0], (slice(None), step(y, 1), pl.ds(6 * QUADS, 2))))
    return stages


def whole_kernel(
    tokens_ref,
    project_in_hbm,
    project_out_hbm,
    expand_hbm,
    reduce_hbm,
    part_hbm,
    tile_ref,
    code_ref,
    first_bias_ref,
    second_hbm,
    second_bias_ref,
    features_hbm,
    out_ref,
    own_ref,
    halo_ref,
    project_in_ref,
    project_out_ref,
    expand_ref,
    reduce_ref,
    kv_own_ref,
    kv_halo_ref,
    query_ref,
    mixed_ref,
    wide_ref,
    small_ref,
    features_ref,
    part_ref,
    whole_ref,
    pooled_ref,
    packed_ref,
    group_ref,
    code_at,
    crops,
    sums_ref,
    ahead_ref,
    passed,
    shares,
    reduced,
    landed,
    parts,
    final,
    second_rows,
    load_sem,
    halo_send,
    halo_recv,
    gather_send,
    gather_recv,
    features_sem,
    swap_send,
    swap_recv,
    pair_send,
    pair_recv,
    row_send,
    row_recv,
    col_send,
    col_recv,
    last_send,
    last_recv,
):
    row, col = lax.axis_index("row"), lax.axis_index("col")
    core = lax.rem(col, 2)
    rows_near = [lax.rem(row + n, ROWS) for n in range(1, ROWS)]
    base = col - core
    stages = gather_stages(row, col, whole_ref, gather_send, gather_recv)

    def remote(source, target, send, recv, to):
        return pltpu.make_async_remote_copy(
            src_ref=source,
            dst_ref=target,
            send_sem=send,
            recv_sem=recv,
            device_id=to,
            device_id_type=MESH,
        )

    def near(dr, dc):
        return lax.rem(row + dr + ROWS, ROWS), lax.rem(col + dc + COLS, COLS)

    barrier = pltpu.get_barrier_semaphore()
    greeted = [near(dr, dc) for dr in (-1, 1) for dc in (-1, 0, 1)] + [near(2, 0)]
    for peer in greeted:
        pl.semaphore_signal(barrier, inc=1, device_id=peer, device_id_type=MESH)

    def greet_col(n, carry):
        pl.semaphore_signal(barrier, inc=1, device_id=near(0, n), device_id_type=MESH)
        return carry

    lax.fori_loop(1, COLS, greet_col, 0)
    loads = [
        pltpu.make_async_copy(source, target, load_sem.at[n])
        for n, (source, target) in enumerate(
            [
                (part_hbm, part_ref),
                (project_in_hbm, project_in_ref),
                (project_out_hbm, project_out_ref),
                (expand_hbm, expand_ref),
                (reduce_hbm, reduce_ref),
            ]
            + [
                (
                    second_hbm.at[pl.ds(row * 256 + k * 64 + h * 32, 32)],
                    second_rows.at[h, pl.ds(k * 32, 32)],
                )
                for h in range(2)
                for k in range(4)
            ]
        )
    ]
    for load in loads:
        load.start()
    for y in range(0, SIDE, 2):
        for a in range(2):
            wide_ref[0:6, a, 0:SIDE, :] = jnp.stack(
                [
                    tokens_ref[y + a, :, n * 128 : (n + 1) * 128].astype(F32)
                    for n in range(6)
                ]
            )
        for strip, cells, x in ((S0, 8, 0), (S1, 16, 7), (S2, 8, 20)):
            own_ref[strip + y * cells : strip + (y + 2) * cells, :] = jnp.concatenate(
                [
                    jnp.concatenate(
                        [wide_ref[n, a, x : x + cells, :] for n in range(6)], axis=1
                    )
                    for a in range(2)
                ],
                axis=0,
            ).astype(BF16)
    pl.semaphore_wait(barrier, len(greeted) + COLS - 1)
    halo_copies = [
        remote(
            own_ref.at[pl.ds(src, rows)],
            halo_ref.at[pl.ds(dst, rows)],
            halo_send.at[n],
            halo_recv.at[n],
            near(dr, dc),
        )
        for n, (src, rows, dst, dr, dc) in enumerate(HALO_COPIES)
    ]
    for copy in halo_copies:
        copy.start()

    z, y = col // 8, lax.rem(col // 2, 4)
    loads[0].wait()

    def pack(q, carry):
        four = [part_ref[4 * q + m].astype(F32) for m in range(4)]
        for m in range(4):
            whole_ref[z, y, 6 * q + m] = four[m][:, :128].astype(BF16)
        for m in range(2):
            whole_ref[z, y, 6 * q + 4 + m] = jnp.concatenate(
                [four[2 * m][:, 128:], four[2 * m + 1][:, 128:]], axis=1
            ).astype(BF16)
        return carry

    lax.fori_loop(0, QUADS, pack, 0)
    last = part_ref[4 * QUADS].astype(F32)
    whole_ref[z, y, 6 * QUADS] = last[:, :128].astype(BF16)
    whole_ref[z, y, 6 * QUADS + 1] = jnp.concatenate(
        [last[:, 128:], jnp.zeros((UNITS, 64), F32)], axis=1
    ).astype(BF16)
    for copy in stages[0]:
        copy.start()

    loads[1].wait()

    def project_own(n, carry):
        at = pl.ds(pl.multiple_of(n * 224, 224), 224)
        normed = norm(own_ref[at, :].astype(F32))
        query_ref[at, :] = (
            jnp.dot(normed, project_in_ref[:, :D], preferred_element_type=F32)
            .astype(BF16)
            .astype(F32)
            * 0.125
        )
        kv_own_ref[at, :] = jnp.dot(
            normed, project_in_ref[:, D:], preferred_element_type=F32
        ).astype(BF16)
        return carry

    lax.fori_loop(0, 4, project_own, 0)
    for copy in halo_copies:
        copy.wait()

    def project_halo(n, carry):
        at = pl.ds(pl.multiple_of(n * 304, 304), 304)
        normed = norm(halo_ref[at, :].astype(F32))
        kv_halo_ref[at, :] = jnp.dot(
            normed, project_in_ref[:, D:], preferred_element_type=F32
        ).astype(BF16)
        return carry

    lax.fori_loop(0, 4, project_halo, 0)
    for copy in stages[0]:
        copy.wait_recv()
    for copy in stages[1]:
        copy.start()

    left_half = lax.broadcasted_iota(jnp.int32, (1, 128), 1) < 64
    ones = jnp.ones((256, 128), BF16)
    for wy in range(3):
        if wy == 1:
            for copy in stages[1]:
                copy.wait_recv()
            for copy in stages[2]:
                copy.start()
        for wx in range(3):
            start, rows = QUERY_ROWS[wy][wx]
            bias = window_bias(wy, wx, row, col)
            pieces = window_keys(wy, wx)
            for h in range(HEADS // 2):
                lanes = slice(h * 128, (h + 1) * 128)
                asked = query_ref[start : start + rows, lanes]
                both = jnp.concatenate(
                    [jnp.where(left_half, asked, 0.0), jnp.where(left_half, 0.0, asked)],
                    axis=0,
                ).astype(BF16)

                def read(first, pieces=pieces):
                    return jnp.concatenate(
                        [
                            (kv_halo_ref if outer else kv_own_ref)[
                                place : place + count, first : first + 128
                            ]
                            for outer, place, count in pieces
                        ],
                        axis=0,
                    )

                scores = (
                    lax.dot_general(
                        both,
                        read(h * 128),
                        (((1,), (1,)), ((), ())),
                        preferred_element_type=F32,
                    )
                    + bias
                )
                weights = jnp.exp(scores - jnp.max(scores, axis=-1, keepdims=True)).astype(BF16)
                values = jnp.concatenate([read(D + h * 128), ones], axis=1)
                mixed = jnp.dot(weights, values, preferred_element_type=F32)
                mixed = mixed[:, :128] / mixed[:, 128:]
                mixed_ref[start : start + rows, lanes] = jnp.where(
                    left_half, mixed[:rows], mixed[rows:]
                )

    for load in loads[2:]:
        load.wait()

    def finish(n, carry):
        at = pl.ds(pl.multiple_of(n * 224, 224), 224)
        after = own_ref[at, :].astype(F32) + jnp.dot(
            mixed_ref[at, :].astype(BF16), project_out_ref[...], preferred_element_type=F32
        )
        normed = norm(after)
        total = after
        for part in range(MLP // D):
            units = slice(part * D, (part + 1) * D)
            hidden = jax.nn.gelu(
                jnp.dot(normed, expand_ref[:, units], preferred_element_type=F32)
            ).astype(BF16)
            total = total + jnp.dot(hidden, reduce_ref[units, :], preferred_element_type=F32)
        mixed_ref[at, :] = total.astype(BF16).astype(F32)
        return carry

    lax.fori_loop(0, 4, finish, 0)

    wide_ref[:, :, SIDE:, :] = jnp.zeros((6, SIDE, 32 - SIDE, 128), F32)

    def place_row(y, carry):
        for n in range(6):
            lanes = slice(n * 128, (n + 1) * 128)
            wide_ref[n, y, 0:8, :] = mixed_ref[pl.ds(pl.multiple_of(S0 + y * 8, 8), 8), lanes]
            wide_ref[n, y, 20:28, :] = mixed_ref[pl.ds(pl.multiple_of(S2 + y * 8, 8), 8), lanes]
            middle = mixed_ref[pl.ds(pl.multiple_of(S1 + y * 16, 16), 16), lanes]
            wide_ref[n, y, 7:21, :] = middle[:14]
        features_ref[y] = jnp.concatenate(
            [wide_ref[n, y, 0:SIDE, :] for n in range(6)], axis=1
        ).astype(BF16)
        return carry

    lax.fori_loop(0, SIDE, place_row, 0)

    def pool(u, carry):
        for n in range(6):
            total = (
                wide_ref[n, 2 * u, pl.ds(0, 16, stride=2), :]
                + wide_ref[n, 2 * u, pl.ds(1, 16, stride=2), :]
                + wide_ref[n, 2 * u + 1, pl.ds(0, 16, stride=2), :]
                + wide_ref[n, 2 * u + 1, pl.ds(1, 16, stride=2), :]
            )
            small_ref[pl.ds(pl.multiple_of(u * 16, 16), 16), n * 128 : (n + 1) * 128] = (
                total * 0.25
            )
        return carry

    lax.fori_loop(0, SIDE // 2, pool, 0)
    features_out = pltpu.make_async_copy(features_ref, features_hbm, features_sem)
    features_out.start()
    near_half = lax.broadcasted_iota(jnp.int32, (112, 128), 1) < 64
    for group, first in enumerate((0, 128, 384, 512)):
        values = small_ref[:, first : first + 256]
        if group % 2:
            values = pltpu.roll(values, 192, 1)
        rest = jnp.where(
            near_half, values[:112, 128:], pltpu.roll(values[112:, 128:], 64, 1)
        )
        pooled_ref[group] = jnp.concatenate(
            [values[:112, :128], values[112:, :128], rest], axis=1
        ).astype(BF16)

    swaps = []
    for n in range(1, ROWS):
        other = lax.rem(row + n, ROWS)
        swaps.append(
            remote(
                pooled_ref.at[other],
                packed_ref.at[core, row],
                swap_send.at[n - 1],
                swap_recv.at[n - 1],
                (other, col),
            )
        )
    for copy in swaps:
        copy.start()
    packed_ref[core, row] = pooled_ref[row]

    def to_pair(n):
        there = lax.rem(row - n + ROWS, ROWS)
        return remote(
            packed_ref.at[core, there],
            packed_ref.at[core, there],
            pair_send.at[n],
            pair_recv.at[n],
            (row, base + 1 - core),
        )

    pairs = [to_pair(n) for n in range(ROWS)]
    pairs[0].start()

    lane = lax.broadcasted_iota(jnp.int32, (COLS, 128), 1)
    for t in range(8):
        here = tile_ref[...] == t // 2 * COLS + base + t % 2
        first = jnp.min(jnp.where(here, lane, 127), axis=1, keepdims=True)
        last = jnp.max(jnp.where(here, lane, 0), axis=1, keepdims=True)
        for rank, pick in enumerate((first, last)):
            code = jnp.sum(jnp.where(lane == pick, code_ref[...], 0), axis=1, keepdims=True)
            code_at[t, rank * COLS : (rank + 1) * COLS, :] = jnp.broadcast_to(code, (COLS, 128))

    tiles = tile_ref[pl.ds(col, 1), :]
    down = lax.broadcasted_iota(jnp.int32, (128, 128), 0)
    across = lax.broadcasted_iota(jnp.int32, (128, 128), 1)
    spread = jnp.broadcast_to(tiles, (128, 128))
    mine = jnp.sum(jnp.where(down == across, spread, 0), axis=1, keepdims=True)
    earlier = jnp.where((mine == spread) & (across < down), 1, 0)
    rank = jnp.max(earlier, axis=1, keepdims=True)
    tile_col = lax.rem(mine, COLS)
    slot = tile_col // 2 * 16 + (mine // COLS * 2 + lax.rem(tile_col, 2)) * 2 + rank
    select = (
        (slot == lax.broadcasted_iota(jnp.int32, (128, 256), 1)).astype(F32).astype(BF16)
    )
    to = lax.broadcasted_iota(jnp.int32, (512, 512), 0)
    source = lax.rem(to // 2, 8) * 64 + lax.rem(to, 2) * 32 + to // 16
    order = (source == lax.broadcasted_iota(jnp.int32, (512, 512), 1)).astype(F32).astype(BF16)

    for n in range(1, ROWS):
        swaps[n - 1].wait_recv()
        pairs[n].start()
    for copy in stages[2]:
        copy.wait_recv()
    for copy in stages[3]:
        copy.start()
    for copy in pairs:
        copy.wait_recv()

    group_ref[:, 224:, :] = jnp.zeros((8, 32, 256), BF16)
    for t in range(8):
        packed = packed_ref[t % 2, t // 2].astype(F32)
        rest = packed[:, 256:]
        turned = pltpu.roll(rest, 64, 1)
        group_ref[t, 0:112, :] = jnp.concatenate(
            [packed[:, :128], jnp.where(near_half, rest, turned)], axis=1
        ).astype(BF16)
        group_ref[t, 112:224, :] = jnp.concatenate(
            [packed[:, 128:256], jnp.where(near_half, turned, rest)], axis=1
        ).astype(BF16)

    spot = lax.broadcasted_iota(jnp.int32, (64, 128), 1)
    near_lanes = spot < 64

    def sample(t, bins):
        code = code_at[t]
        below = 16 * (1 + lax.rem(code // 2, 2))
        right = 1 + lax.rem(code, 2)
        picks = []
        for bin in bins:
            position = code // 4 + (bin // 7) * below + (bin % 7) * right
            low = (position == spot).astype(F32)
            high = (position == spot + 128).astype(F32)
            picks.append(jnp.concatenate([low, high], axis=1).astype(BF16))
        return jnp.dot(
            jnp.concatenate(picks, axis=0), group_ref[t], preferred_element_type=F32
        )

    def multiply(width, tile):
        weight = jnp.concatenate(
            [whole_ref[:, :, tile + n].reshape(16 * UNITS, 128) for n in range(width)], axis=1
        )
        return lax.dot_general(
            crops[:, : 128 * width],
            weight,
            (((1,), (1,)), ((), ())),
            preferred_element_type=F32,
        )

    stages[3][12].wait_recv()
    for t in range(8):
        crops[t * 64 : (t + 1) * 64, :256] = sample(t, (4 * QUADS,)).astype(BF16)
    total = mixed_ref.at[0:512, 0:512]
    total[...] = multiply(2, 6 * QUADS)
    for n in range(3):
        for quarter in range(4):
            quad = 3 * quarter + n
            for t in range(8):
                found = sample(t, range(4 * quad, 4 * quad + 4))
                for m in range(4):
                    crops[t * 64 : (t + 1) * 64, m * 128 : (m + 1) * 128] = found[
                        m * 64 : (m + 1) * 64, :128
                    ].astype(BF16)
                for m in range(2):
                    crops[t * 64 : (t + 1) * 64, (4 + m) * 128 : (5 + m) * 128] = jnp.where(
                        near_lanes,
                        found[m * 128 : m * 128 + 64, 128:],
                        found[m * 128 + 64 : m * 128 + 128, 128:],
                    ).astype(BF16)
            stages[3][4 * n + quarter].wait_recv()
            total[...] += multiply(6, 6 * quad)
    sums_ref[...] = jnp.dot(
        order, total[...].astype(BF16), preferred_element_type=F32
    ).astype(BF16)

    def share(n):
        return pl.ds(pl.multiple_of(lax.rem(row + n + ROWS, ROWS) * 128, 128), 128)

    sides = ((1, 0), (-1, 256))
    far = [
        remote(
            sums_ref.at[pl.ds(first, 256), share(2)],
            passed.at[n],
            row_send.at[n],
            row_recv.at[n],
            near(dr, 0),
        )
        for n, (dr, first) in enumerate(sides)
    ]
    for copy in far:
        copy.start()
    for copy in far:
        copy.wait_recv()
    close = []
    for n, (dr, first) in enumerate(sides):
        ahead_ref[n] = sums_ref[:, share(dr)]
        ahead_ref[n, first : first + 256, :] = (
            sums_ref[first : first + 256, share(dr)].astype(F32) + passed[n].astype(F32)
        ).astype(BF16)
        close.append(
            remote(ahead_ref.at[n], shares.at[n], row_send.at[2 + n], row_recv.at[2 + n], near(dr, 0))
        )
        close[n].start()
    for copy in close:
        copy.wait_recv()
    summed = sums_ref[:, share(0)].astype(F32) + shares[0].astype(F32) + shares[1].astype(F32)
    reduced[...] = summed.astype(BF16)

    def to_col(n):
        other = lax.rem(col + n, COLS)
        return pltpu.make_async_remote_copy(
            src_ref=reduced.at[pl.ds(pl.multiple_of(other * 16, 16), 16)],
            dst_ref=landed.at[col],
            send_sem=col_send.at[n],
            recv_sem=col_recv.at[n],
            device_id=(row, other),
            device_id_type=MESH,
        )

    def start_col(n, carry):
        to_col(n).start()
        return carry

    lax.fori_loop(1, COLS, start_col, 0)
    landed[col] = reduced[pl.ds(pl.multiple_of(col * 16, 16), 16), :]

    def wait_col(n, carry):
        to_col(n).wait()
        return carry

    lax.fori_loop(1, COLS, wait_col, 0)
    second = None
    for h in range(2):
        slots = jnp.concatenate([landed[2 * k + h] for k in range(16)], axis=0)
        chosen = jnp.dot(select, slots, preferred_element_type=F32)
        hidden = jnp.maximum(chosen + first_bias_ref[row, h : h + 1, :], 0.0).astype(BF16)
        part = jnp.dot(hidden, second_rows[h], preferred_element_type=F32)
        second = part if second is None else second + part
    parts[...] = second.astype(BF16)
    copies = [
        pltpu.make_async_remote_copy(
            src_ref=parts.at[:, pl.ds(pl.multiple_of(other * 256, 256), 256)],
            dst_ref=final.at[n],
            send_sem=last_send.at[n],
            recv_sem=last_recv.at[n],
            device_id=(other, col),
            device_id_type=MESH,
        )
        for n, other in enumerate(rows_near)
    ]
    for copy in copies:
        copy.start()
    for copy in copies:
        copy.wait()
    summed = parts[:, pl.ds(pl.multiple_of(row * 256, 256), 256)].astype(F32)
    for n in range(ROWS - 1):
        summed = summed + final[n].astype(F32)
    out_ref[...] = jnp.maximum(summed + second_bias_ref[pl.ds(row, 1), :], 0.0).astype(BF16)
    for stage in stages:
        for copy in stage:
            copy.wait_send()
    for copy in swaps + pairs + far + close:
        copy.wait_send()
    features_out.wait()


def whole(
    tokens,
    project_in,
    project_out,
    expand_weight,
    reduce_weight,
    first_weight,
    tiles,
    codes,
    first_bias,
    second_weight,
    second_bias,
):
    anywhere = pl.BlockSpec(memory_space=pl.ANY)
    dma = pltpu.SemaphoreType.DMA
    halo_count = len(HALO_COPIES)
    return pl.pallas_call(
        whole_kernel,
        out_shape=(
            jax.ShapeDtypeStruct((SIDE, SIDE, D), BF16),
            jax.ShapeDtypeStruct((128, 256), BF16),
        ),
        in_specs=[VMEM_SPEC]
        + [anywhere] * 5
        + [VMEM_SPEC] * 3
        + [anywhere, VMEM_SPEC],
        out_specs=(anywhere, VMEM_SPEC),
        scratch_shapes=[
            pltpu.VMEM((OWN, D), BF16),
            pltpu.VMEM((HALO, D), BF16),
            pltpu.VMEM((D, 3 * D), BF16),
            pltpu.VMEM((D, D), BF16),
            pltpu.VMEM((D, MLP), BF16),
            pltpu.VMEM((MLP, D), BF16),
            pltpu.VMEM((OWN, 2 * D), BF16),
            pltpu.VMEM((HALO, 2 * D), BF16),
            pltpu.VMEM((OWN, D), F32),
            pltpu.VMEM((OWN, D), F32),
            pltpu.VMEM((6, SIDE, 32, 128), F32),
            pltpu.VMEM((224, D), F32),
            pltpu.VMEM((SIDE, SIDE, D), BF16),
            pltpu.VMEM((49, UNITS, 192), BF16),
            pltpu.VMEM((4, 4, TILES, UNITS, 128), BF16),
            pltpu.VMEM((ROWS, 112, 384), BF16),
            pltpu.VMEM((2, ROWS, 112, 384), BF16),
            pltpu.VMEM((8, 256, 256), BF16),
            pltpu.VMEM((8, 64, 128), jnp.int32),
            pltpu.VMEM((512, D), BF16),
            pltpu.VMEM((512, 512), BF16),
            pltpu.VMEM((2, 512, 128), BF16),
            pltpu.VMEM((2, 256, 128), BF16),
            pltpu.VMEM((2, 512, 128), BF16),
            pltpu.VMEM((512, 128), BF16),
            pltpu.VMEM((COLS, 16, 128), BF16),
            pltpu.VMEM((128, FC), BF16),
            pltpu.VMEM((ROWS - 1, 128, 256), BF16),
            pltpu.VMEM((2, 128, FC), BF16),
            dma((13,)),
            dma((halo_count,)),
            dma((halo_count,)),
            dma((GATHER,)),
            dma((GATHER,)),
            dma,
            dma((ROWS - 1,)),
            dma((ROWS - 1,)),
            dma((ROWS,)),
            dma((ROWS,)),
            dma((4,)),
            dma((4,)),
            dma((COLS,)),
            dma((COLS,)),
            dma((ROWS - 1,)),
            dma((ROWS - 1,)),
        ],
        compiler_params=pltpu.CompilerParams(
            collective_id=0, has_side_effects=True, vmem_limit_bytes=62 * 1024 * 1024
        ),
        cost_estimate=pl.CostEstimate(
            flops=27_000_000_000, bytes_accessed=34_000_000, transcendentals=6_000_000
        ),
        name="whole",
    )(
        tokens,
        project_in,
        project_out,
        expand_weight,
        reduce_weight,
        first_weight,
        tiles,
        codes,
        first_bias,
        second_weight,
        second_bias,
    )


def shards(
    tokens,
    project_in,
    project_out,
    expand_weight,
    reduce_weight,
    first_weight,
    first_bias,
    second_weight,
    second_bias,
    box_tile,
    box_shape,
):
    tiles = box_tile.reshape(COLS, 128)
    codes = (
        (box_shape[:, 0] * 16 + box_shape[:, 1]) * 4
        + (box_shape[:, 2] - 1) * 2
        + (box_shape[:, 3] - 1)
    ).reshape(COLS, 128)
    bias = first_bias.reshape(ROWS, 4, 2, 32).transpose(0, 2, 1, 3).reshape(ROWS, 2, 128)
    features, box_features = whole(
        tokens,
        project_in,
        project_out,
        expand_weight,
        reduce_weight,
        first_weight.transpose(0, 2, 1),
        tiles,
        codes,
        bias,
        second_weight,
        second_bias.reshape(ROWS, 256),
    )
    return (features, box_features)


def solution(mesh):
    return jax.shard_map(
        shards,
        mesh=mesh,
        in_specs=(
            P("row", "col", None),
            P(),
            P(),
            P(),
            P(),
            P(None, "row", "col"),
            P(),
            P(),
            P(),
            P(),
            P(),
        ),
        out_specs=(P("row", "col", None), P("col", "row")),
        check_vma=False,
    )
```

time: 151 us -> 122 us (0.81)
  Pallas kernels: 145 us -> 113 us
  local copies, waits for them, and re-layouts: 3.09 us -> 5.91 us
    pallas_call x2 -> x1, Pallas kernels: 145 us -> 113 us  [whole(): pl.pallas_call(whole_kernel, out_shape=(jax.ShapeDtypeStruct((SIDE, SIDE,...]
    unnamed x12 -> x4, local copies, waits for them, and re-layouts: 1.73 us -> 3.17 us
where the time goes in v3:
time: 122 us; the launch traced here: 121 us
  Pallas kernels  113 us (93%)
  local copies, waits for them, and re-layouts  5.91 us (5%)
  other arithmetic  1.66 us (1%)
    pallas_call x1, Pallas kernels, whole(): pl.pallas_call(whole_kernel, out_shape=(jax.ShapeDtypeStruct((SIDE, SIDE,...  113 us
    unnamed x4, local copies, waits for them, and re-layouts  3.17 us

profile of v3, /device:TPU:0, one launch (start us, length us, event | category | flops | bytes accessed | tf_op | source)
XLA Modules:
  0.0 121.4 jit_solution(2339063725282197348)
XLA Ops:
  0.6 1.3 %reshape.36.second_bias_ref = f32[4,256]{1,0:T(4,128)} reshape(f32[1024]{0:T(1024)} %param.19) | data formatting | bytes 8192 | tf_op jit(solution)/shard_map/reshape | solution.py:803
  1.9 0.8 reshape.34
  2.7 0.7 reshape.35.first_bias_ref
  3.4 1.7 %add_add_fusion = s32[4096,1]{0,1:T(1,128)} fusion(s32[4096,4]{0,1:T(4,128)} %param.21), kind=kLoop, calls=%fused_computation | loop fusion | flops 32768 | bytes 81920 | tf_op jit(solution)/shard_map/add | solution.py:787
  5.0 113.2 %whole.1 = (bf16[28,28,768]{2,1,0:T(8,128)(2,1)}, bf16[128,256]{1,0:T(8,128)(2,1)}) custom-call(bf16[28,28,768]{2,1,0:T(8,128)(2,1)} %tokens_ref.1, bf16[768,2304]{1,0:T(8,128)(2,1)} %project_in_hbm.1, bf16[768,768]{1,0:T(8,128)(2,1)} %project_out_hbm.1, bf16[768,3072]{1,0:T(8,128)(2,1)} %expand_hbm.1, bf16[3072,768]{1,0:T(8,128)(2,1)} %reduce_hbm.1, ...), custom_call_target="tpu_custom_call" | custom-call | flops 27000000512 | bytes 34000000 | tf_op jit(solution)/shard_map/whole/pallas_call | solution.py:692
  118.2 0.0 copy-start
  118.2 2.5 %copy.16 = bf16[28,28,768]{2,1,0:T(8,128)(2,1)} copy(bf16[28,28,768]{2,1,0:T(8,128)(2,1)} %get-tuple-element.4) | data formatting | bytes 2408448
  120.8 0.0 copy-done
  120.8 0.6 copy.17
  (1 shorter events, 0.0 us)
Async XLA Ops:
  118.2 2.5 %copy-start = (bf16[128,256]{1,0:T(8,128)(2,1)S(1)}, bf16[128,256]{1,0:T(8,128)(2,1)}, u32[]{:S(2)}) copy-start(bf16[128,256]{1,0:T(8,128)(2,1)} %get-tuple-element.5) | copy-start | bytes 196612

commit v4 on v3

--- a/solution.py
+++ b/solution.py
@@ -32,7 +32,7 @@
 TILES = 6 * QUADS + 2
 HALVES = ((0, 36), (36, 38))
 QUARTERS = ((0, 18), (18, 18), (36, 18), (54, 20))
-GATHER = 25
+GATHER = 49
 UNITS = 32
 MESH = pl.DeviceIdType.MESH
 F32 = jnp.float32
@@ -113,30 +113,46 @@
     def step(at, by):
         return lax.rem(at + by + 4, 4)
 
-    up = [device(0, 1), device(1, 0)]
-    down = [device(0, -1), device(-1, 0)]
-    stages = [[], [], [], []]
-    for axis in range(2):
-        for to in (up[axis], down[axis]):
-            stages[0].append(send(to, (z, y, pl.ds(*HALVES[axis]))))
-    for axis in range(2):
-        for sign, to, part in ((-1, up[axis], 0), (1, down[axis], 1)):
-            chunk = (z, step(y, sign)) if axis == 0 else (step(z, sign), y)
-            stages[1].append(send(to, (*chunk, pl.ds(*QUARTERS[2 * axis + part]))))
-    for to in (up[1], down[1]):
-        stages[2].append(send(to, (z, slice(None), pl.ds(*HALVES[0]))))
-    for to in (up[0], down[0]):
-        stages[2].append(send(to, (slice(None), y, pl.ds(*HALVES[1]))))
+    def chunk(axis, first, second):
+        dz, dy = (second, first) if axis == 0 else (first, second)
+        return step(z, dz), step(y, dy)
+
+    first_to = [{1: device(0, 1), -1: device(0, -1)}, {1: device(1, 0), -1: device(-1, 0)}]
+    second_to = first_to[::-1]
+
+    def part(axis, sign):
+        return QUARTERS[2 * axis + (0 if sign == 1 else 1)]
+
+    both = [(axis, sign) for axis in range(2) for sign in (1, -1)]
+    stages = {n: [] for n in ("own", "cross", "on", "near", "far", "over", "last", "end")}
+    for axis, sign in both:
+        whole = pl.ds(*HALVES[axis])
+        stages["own"].append(send(first_to[axis][sign], (*chunk(axis, 0, 0), whole)))
+    for axis, sign in both:
+        whole = pl.ds(*HALVES[axis])
+        stages["cross"].append(send(second_to[axis][sign], (*chunk(axis, 0, 0), whole)))
+    for axis, sign in both:
+        place = (*chunk(axis, -sign, 0), pl.ds(*part(axis, sign)))
+        stages["on"].append(send(first_to[axis][sign], place))
+    for off in (1, -1):
+        for axis, sign in both:
+            place = (*chunk(axis, off, 0), pl.ds(*HALVES[axis]))
+            stages["near"].append(send(second_to[axis][sign], place))
+    for axis, sign in both:
+        place = (*chunk(axis, 0, -sign), pl.ds(*part(axis, sign)))
+        stages["far"].append(send(second_to[axis][sign], place))
+    for axis, sign in both:
+        place = (*chunk(axis, 2, 0), pl.ds(*HALVES[axis]))
+        stages["over"].append(send(second_to[axis][sign], place))
+    for off in (1, -1):
+        for axis, sign in both:
+            place = (*chunk(axis, off, -sign), pl.ds(*part(axis, sign)))
+            stages["last"].append(send(second_to[axis][sign], place))
     for n in range(3):
-        for quarter in range(4):
-            sign, to = ((-1, up), (1, down))[quarter % 2]
-            tiles = pl.ds(QUARTERS[quarter][0] + 6 * n, 6)
-            if quarter < 2:
-                place = (step(z, sign), slice(None), tiles)
-            else:
-                place = (slice(None), step(y, sign), tiles)
-            stages[3].append(send(to[1 - quarter // 2], place))
-    stages[3].append(send(down[0], (slice(None), step(y, 1), pl.ds(6 * QUADS, 2))))
+        for axis, sign in both:
+            place = (*chunk(axis, 2, -sign), pl.ds(part(axis, sign)[0] + 6 * n, 6))
+            stages["end"].append(send(second_to[axis][sign], place))
+    stages["end"].append(send(second_to[1][-1], (*chunk(1, 2, 1), pl.ds(6 * QUADS, 2))))
     return stages
 
 
@@ -148,11 +164,11 @@
     reduce_hbm,
     part_hbm,
     tile_ref,
-    code_ref,
+    shape_ref,
     first_bias_ref,
     second_hbm,
     second_bias_ref,
-    features_hbm,
+    features_ref,
     out_ref,
     own_ref,
     halo_ref,
@@ -166,12 +182,12 @@
     mixed_ref,
     wide_ref,
     small_ref,
-    features_ref,
     part_ref,
     whole_ref,
     pooled_ref,
     packed_ref,
     group_ref,
+    code_ref,
     code_at,
     crops,
     sums_ref,
@@ -188,7 +204,6 @@
     halo_recv,
     gather_send,
     gather_recv,
-    features_sem,
     swap_send,
     swap_recv,
     pair_send,
@@ -302,7 +317,7 @@
     whole_ref[z, y, 6 * QUADS + 1] = jnp.concatenate(
         [last[:, 128:], jnp.zeros((UNITS, 64), F32)], axis=1
     ).astype(BF16)
-    for copy in stages[0]:
+    for copy in stages["own"] + stages["cross"]:
         copy.start()
 
     loads[1].wait()
@@ -322,78 +337,58 @@
         return carry
 
     lax.fori_loop(0, 4, project_own, 0)
-    for copy in halo_copies:
-        copy.wait()
-
-    def project_halo(n, carry):
-        at = pl.ds(pl.multiple_of(n * 304, 304), 304)
-        normed = norm(halo_ref[at, :].astype(F32))
-        kv_halo_ref[at, :] = jnp.dot(
-            normed, project_in_ref[:, D:], preferred_element_type=F32
-        ).astype(BF16)
-        return carry
-
-    lax.fori_loop(0, 4, project_halo, 0)
-    for copy in stages[0]:
-        copy.wait_recv()
-    for copy in stages[1]:
-        copy.start()
-
     left_half = lax.broadcasted_iota(jnp.int32, (1, 128), 1) < 64
     ones = jnp.ones((256, 128), BF16)
-    for wy in range(3):
-        if wy == 1:
-            for copy in stages[1]:
-                copy.wait_recv()
-            for copy in stages[2]:
-                copy.start()
-        for wx in range(3):
-            start, rows = QUERY_ROWS[wy][wx]
-            bias = window_bias(wy, wx, row, col)
-            pieces = window_keys(wy, wx)
-            for h in range(HEADS // 2):
-                lanes = slice(h * 128, (h + 1) * 128)
-                asked = query_ref[start : start + rows, lanes]
-                both = jnp.concatenate(
-                    [jnp.where(left_half, asked, 0.0), jnp.where(left_half, 0.0, asked)],
+
+    def attend(wy, wx):
+        start, rows = QUERY_ROWS[wy][wx]
+        bias = window_bias(wy, wx, row, col)
+        pieces = window_keys(wy, wx)
+        for h in range(HEADS // 2):
+            lanes = slice(h * 128, (h + 1) * 128)
+            asked = query_ref[start : start + rows, lanes]
+            both = jnp.concatenate(
+                [jnp.where(left_half, asked, 0.0), jnp.where(left_half, 0.0, asked)],
+                axis=0,
+            ).astype(BF16)
+
+            def read(first, pieces=pieces):
+                return jnp.concatenate(
+                    [
+                        (kv_halo_ref if outer else kv_own_ref)[
+                            place : place + count, first : first + 128
+                        ]
+                        for outer, place, count in pieces
+                    ],
                     axis=0,
-                ).astype(BF16)
-
-                def read(first, pieces=pieces):
-                    return jnp.concatenate(
-                        [
-                            (kv_halo_ref if outer else kv_own_ref)[
-                                place : place + count, first : first + 128
-                            ]
-                            for outer, place, count in pieces
-                        ],
-                        axis=0,
-                    )
-
-                scores = (
-                    lax.dot_general(
-                        both,
-                        read(h * 128),
-                        (((1,), (1,)), ((), ())),
-                        preferred_element_type=F32,
-                    )
-                    + bias
                 )
-                weights = jnp.exp(scores - jnp.max(scores, axis=-1, keepdims=True)).astype(BF16)
-                values = jnp.concatenate([read(D + h * 128), ones], axis=1)
-                mixed = jnp.dot(weights, values, preferred_element_type=F32)
-                mixed = mixed[:, :128] / mixed[:, 128:]
-                mixed_ref[start : start + rows, lanes] = jnp.where(
-                    left_half, mixed[:rows], mixed[rows:]
+
+            scores = (
+                lax.dot_general(
+                    both,
+                    read(h * 128),
+                    (((1,), (1,)), ((), ())),
+                    preferred_element_type=F32,
                 )
-
-    for load in loads[2:]:
-        load.wait()
-
-    def finish(n, carry):
-        at = pl.ds(pl.multiple_of(n * 224, 224), 224)
-        after = own_ref[at, :].astype(F32) + jnp.dot(
-            mixed_ref[at, :].astype(BF16), project_out_ref[...], preferred_element_type=F32
+                + bias
+            )
+            weights = jnp.exp(scores - jnp.max(scores, axis=-1, keepdims=True)).astype(BF16)
+            values = jnp.concatenate([read(D + h * 128), ones], axis=1)
+            mixed = jnp.dot(weights, values, preferred_element_type=F32)
+            mixed = mixed[:, :128] / mixed[:, 128:]
+            mixed_ref[start : start + rows, lanes] = jnp.where(
+                left_half, mixed[:rows], mixed[rows:]
+            )
+
+    def finish(spans):
+        after = jnp.concatenate(
+            [own_ref[first : first + rows, :].astype(F32) for first, rows in spans], axis=0
+        ) + jnp.dot(
+            jnp.concatenate(
+                [mixed_ref[first : first + rows, :].astype(BF16) for first, rows in spans], axis=0
+            ),
+            project_out_ref[...],
+            preferred_element_type=F32,
         )
         normed = norm(after)
         total = after
@@ -403,83 +398,28 @@
                 jnp.dot(normed, expand_ref[:, units], preferred_element_type=F32)
             ).astype(BF16)
             total = total + jnp.dot(hidden, reduce_ref[units, :], preferred_element_type=F32)
-        mixed_ref[at, :] = total.astype(BF16).astype(F32)
-        return carry
-
-    lax.fori_loop(0, 4, finish, 0)
-
-    wide_ref[:, :, SIDE:, :] = jnp.zeros((6, SIDE, 32 - SIDE, 128), F32)
-
-    def place_row(y, carry):
-        for n in range(6):
-            lanes = slice(n * 128, (n + 1) * 128)
-            wide_ref[n, y, 0:8, :] = mixed_ref[pl.ds(pl.multiple_of(S0 + y * 8, 8), 8), lanes]
-            wide_ref[n, y, 20:28, :] = mixed_ref[pl.ds(pl.multiple_of(S2 + y * 8, 8), 8), lanes]
-            middle = mixed_ref[pl.ds(pl.multiple_of(S1 + y * 16, 16), 16), lanes]
-            wide_ref[n, y, 7:21, :] = middle[:14]
-        features_ref[y] = jnp.concatenate(
-            [wide_ref[n, y, 0:SIDE, :] for n in range(6)], axis=1
-        ).astype(BF16)
-        return carry
-
-    lax.fori_loop(0, SIDE, place_row, 0)
-
-    def pool(u, carry):
-        for n in range(6):
-            total = (
-                wide_ref[n, 2 * u, pl.ds(0, 16, stride=2), :]
-                + wide_ref[n, 2 * u, pl.ds(1, 16, stride=2), :]
-                + wide_ref[n, 2 * u + 1, pl.ds(0, 16, stride=2), :]
-                + wide_ref[n, 2 * u + 1, pl.ds(1, 16, stride=2), :]
-            )
-            small_ref[pl.ds(pl.multiple_of(u * 16, 16), 16), n * 128 : (n + 1) * 128] = (
-                total * 0.25
-            )
-        return carry
-
-    lax.fori_loop(0, SIDE // 2, pool, 0)
-    features_out = pltpu.make_async_copy(features_ref, features_hbm, features_sem)
-    features_out.start()
-    near_half = lax.broadcasted_iota(jnp.int32, (112, 128), 1) < 64
-    for group, first in enumerate((0, 128, 384, 512)):
-        values = small_ref[:, first : first + 256]
-        if group % 2:
-            values = pltpu.roll(values, 192, 1)
-        rest = jnp.where(
-            near_half, values[:112, 128:], pltpu.roll(values[112:, 128:], 64, 1)
-        )
-        pooled_ref[group] = jnp.concatenate(
-            [values[:112, :128], values[112:, :128], rest], axis=1
-        ).astype(BF16)
-
-    swaps = []
-    for n in range(1, ROWS):
-        other = lax.rem(row + n, ROWS)
-        swaps.append(
-            remote(
-                pooled_ref.at[other],
-                packed_ref.at[core, row],
-                swap_send.at[n - 1],
-                swap_recv.at[n - 1],
-                (other, col),
-            )
-        )
-    for copy in swaps:
+        total = total.astype(BF16).astype(F32)
+        done = 0
+        for first, rows in spans:
+            mixed_ref[first : first + rows, :] = total[done : done + rows]
+            done += rows
+
+    attend(1, 1)
+    for load in loads[2:]:
+        load.wait()
+    finish(((S1 + 112, 224),))
+    for copy in stages["own"]:
+        copy.wait_recv()
+    for copy in stages["on"] + stages["near"]:
         copy.start()
-    packed_ref[core, row] = pooled_ref[row]
-
-    def to_pair(n):
-        there = lax.rem(row - n + ROWS, ROWS)
-        return remote(
-            packed_ref.at[core, there],
-            packed_ref.at[core, there],
-            pair_send.at[n],
-            pair_recv.at[n],
-            (row, base + 1 - core),
-        )
-
-    pairs = [to_pair(n) for n in range(ROWS)]
-    pairs[0].start()
+
+    for c in range(COLS):
+        lanes = slice(c * 128, (c + 1) * 128)
+        code_ref[c : c + 1, :] = (
+            (shape_ref[0:1, lanes] * 16 + shape_ref[1:2, lanes]) * 4
+            + (shape_ref[2:3, lanes] - 1) * 2
+            + (shape_ref[3:4, lanes] - 1)
+        )
 
     lane = lax.broadcasted_iota(jnp.int32, (COLS, 128), 1)
     for t in range(8):
@@ -506,27 +446,135 @@
     source = lax.rem(to // 2, 8) * 64 + lax.rem(to, 2) * 32 + to // 16
     order = (source == lax.broadcasted_iota(jnp.int32, (512, 512), 1)).astype(F32).astype(BF16)
 
-    for n in range(1, ROWS):
-        swaps[n - 1].wait_recv()
-        pairs[n].start()
-    for copy in stages[2]:
+    for copy in halo_copies:
+        copy.wait()
+
+    def project_halo(n, carry):
+        at = pl.ds(pl.multiple_of(n * 304, 304), 304)
+        normed = norm(halo_ref[at, :].astype(F32))
+        kv_halo_ref[at, :] = jnp.dot(
+            normed, project_in_ref[:, D:], preferred_element_type=F32
+        ).astype(BF16)
+        return carry
+
+    lax.fori_loop(0, 4, project_halo, 0)
+    for copy in stages["cross"]:
         copy.wait_recv()
-    for copy in stages[3]:
+    for copy in stages["far"]:
         copy.start()
+
+    for wy in range(3):
+        for wx in range(3):
+            if (wy, wx) != (1, 1):
+                attend(wy, wx)
+
+    for copy in stages["on"]:
+        copy.wait_recv()
+    for copy in stages["over"]:
+        copy.start()
+
+    wide_ref[:, :, SIDE:, :] = jnp.zeros((6, SIDE, 32 - SIDE, 128), F32)
+
+    def place_row(y, carry):
+        for n in range(6):
+            lanes = slice(n * 128, (n + 1) * 128)
+            wide_ref[n, y, 0:8, :] = mixed_ref[pl.ds(pl.multiple_of(S0 + y * 8, 8), 8), lanes]
+            wide_ref[n, y, 20:28, :] = mixed_ref[pl.ds(pl.multiple_of(S2 + y * 8, 8), 8), lanes]
+            middle = mixed_ref[pl.ds(pl.multiple_of(S1 + y * 16, 16), 16), lanes]
+            wide_ref[n, y, 7:21, :] = middle[:14]
+        features_ref[y] = jnp.concatenate(
+            [wide_ref[n, y, 0:SIDE, :] for n in range(6)], axis=1
+        ).astype(BF16)
+        return carry
+
+    def pool(u, carry):
+        for n in range(6):
+            total = (
+                wide_ref[n, 2 * u, pl.ds(0, 16, stride=2), :]
+                + wide_ref[n, 2 * u, pl.ds(1, 16, stride=2), :]
+                + wide_ref[n, 2 * u + 1, pl.ds(0, 16, stride=2), :]
+                + wide_ref[n, 2 * u + 1, pl.ds(1, 16, stride=2), :]
+            )
+            small_ref[pl.ds(pl.multiple_of(u * 16, 16), 16), n * 128 : (n + 1) * 128] = (
+                total * 0.25
+            )
+        return carry
+
+    near_half = lax.broadcasted_iota(jnp.int32, (64, 128), 1) < 64
+
+    def pack_pooled(half):
+        for group, first in enumerate((0, 128, 384, 512)):
+            values = small_ref[half * 112 : half * 112 + 112, first : first + 256]
+            if group % 2:
+                values = pltpu.roll(values, 192, 1)
+            upper, lower = values[:64], values[48:]
+            rest = jnp.where(near_half, upper[:, 128:], pltpu.roll(lower[:, 128:], 64, 1))
+            pooled_ref[half, group] = jnp.concatenate(
+                [upper[:, :128], lower[:, :128], rest], axis=1
+            ).astype(BF16)
+
+    def to_row(half, n):
+        other = lax.rem(row + n, ROWS)
+        return remote(
+            pooled_ref.at[half, other],
+            packed_ref.at[half, core, row],
+            swap_send.at[half * 3 + n - 1],
+            swap_recv.at[half * 3 + n - 1],
+            (other, col),
+        )
+
+    def to_pair(half, n):
+        there = lax.rem(row - n + ROWS, ROWS)
+        return remote(
+            packed_ref.at[half, core, there],
+            packed_ref.at[half, core, there],
+            pair_send.at[half * 4 + n],
+            pair_recv.at[half * 4 + n],
+            (row, base + 1 - core),
+        )
+
+    swaps = [[to_row(half, n) for n in range(1, ROWS)] for half in range(2)]
+    pairs = [[to_pair(half, n) for n in range(ROWS)] for half in range(2)]
+    for half in range(2):
+        finish(((S0 + half * 112, 112), (S1 + half * 336, 112), (S2 + half * 112, 112)))
+        if half == 1:
+            for copy in stages["near"]:
+                copy.wait_recv()
+            for copy in stages["last"]:
+                copy.start()
+        lax.fori_loop(half * 14, half * 14 + 14, place_row, 0)
+        lax.fori_loop(half * 7, half * 7 + 7, pool, 0)
+        pack_pooled(half)
+        for copy in swaps[half]:
+            copy.start()
+        packed_ref[half, core, row] = pooled_ref[half, row]
+        pairs[half][0].start()
+    for half in range(2):
+        for n in range(1, ROWS):
+            swaps[half][n - 1].wait_recv()
+            pairs[half][n].start()
+    for copy in stages["over"]:
+        copy.wait_recv()
+    for copy in stages["end"]:
+        copy.start()
+    swaps = swaps[0] + swaps[1]
+    pairs = pairs[0] + pairs[1]
     for copy in pairs:
         copy.wait_recv()
 
     group_ref[:, 224:, :] = jnp.zeros((8, 32, 256), BF16)
-    for t in range(8):
-        packed = packed_ref[t % 2, t // 2].astype(F32)
-        rest = packed[:, 256:]
-        turned = pltpu.roll(rest, 64, 1)
-        group_ref[t, 0:112, :] = jnp.concatenate(
-            [packed[:, :128], jnp.where(near_half, rest, turned)], axis=1
-        ).astype(BF16)
-        group_ref[t, 112:224, :] = jnp.concatenate(
-            [packed[:, 128:256], jnp.where(near_half, turned, rest)], axis=1
-        ).astype(BF16)
+    for half in range(2):
+        top = half * 112
+        for t in range(8):
+            packed = packed_ref[half, t % 2, t // 2].astype(F32)
+            rest = packed[:, 256:]
+            turned = pltpu.roll(rest, 64, 1)
+            group_ref[t, top : top + 64, :] = jnp.concatenate(
+                [packed[:, :128], jnp.where(near_half, rest, turned)], axis=1
+            ).astype(BF16)
+            group_ref[t, top + 48 : top + 112, :] = jnp.concatenate(
+                [packed[:, 128:256], jnp.where(near_half, turned, rest)], axis=1
+            ).astype(BF16)
 
     spot = lax.broadcasted_iota(jnp.int32, (64, 128), 1)
     near_lanes = spot < 64
@@ -556,7 +604,8 @@
             preferred_element_type=F32,
         )
 
-    stages[3][12].wait_recv()
+    for copy in stages["far"] + stages["last"] + stages["end"][12:]:
+        copy.wait_recv()
     for t in range(8):
         crops[t * 64 : (t + 1) * 64, :256] = sample(t, (4 * QUADS,)).astype(BF16)
     total = mixed_ref.at[0:512, 0:512]
@@ -576,7 +625,7 @@
                         found[m * 128 : m * 128 + 64, 128:],
                         found[m * 128 + 64 : m * 128 + 128, 128:],
                     ).astype(BF16)
-            stages[3][4 * n + quarter].wait_recv()
+            stages["end"][4 * n + quarter].wait_recv()
             total[...] += multiply(6, 6 * quad)
     sums_ref[...] = jnp.dot(
         order, total[...].astype(BF16), preferred_element_type=F32
@@ -642,7 +691,15 @@
     for h in range(2):
         slots = jnp.concatenate([landed[2 * k + h] for k in range(16)], axis=0)
         chosen = jnp.dot(select, slots, preferred_element_type=F32)
-        hidden = jnp.maximum(chosen + first_bias_ref[row, h : h + 1, :], 0.0).astype(BF16)
+        bias = jnp.concatenate(
+            [
+                first_bias_ref[pl.ds(2 * row + n, 1), :][:, 64 * m + 32 * h : 64 * m + 32 * h + 32]
+                for n in range(2)
+                for m in range(2)
+            ],
+            axis=1,
+        )
+        hidden = jnp.maximum(chosen + bias, 0.0).astype(BF16)
         part = jnp.dot(hidden, second_rows[h], preferred_element_type=F32)
         second = part if second is None else second + part
     parts[...] = second.astype(BF16)
@@ -664,13 +721,13 @@
     summed = parts[:, pl.ds(pl.multiple_of(row * 256, 256), 256)].astype(F32)
     for n in range(ROWS - 1):
         summed = summed + final[n].astype(F32)
-    out_ref[...] = jnp.maximum(summed + second_bias_ref[pl.ds(row, 1), :], 0.0).astype(BF16)
-    for stage in stages:
+    bias = jnp.concatenate([second_bias_ref[pl.ds(2 * row + n, 1), :] for n in range(2)], axis=1)
+    out_ref[...] = jnp.maximum(summed + bias, 0.0).astype(BF16)
+    for stage in stages.values():
         for copy in stage:
             copy.wait_send()
     for copy in swaps + pairs + far + close:
         copy.wait_send()
-    features_out.wait()
 
 
 def whole(
@@ -681,7 +738,7 @@
     reduce_weight,
     first_weight,
     tiles,
-    codes,
+    shapes,
     first_bias,
     second_weight,
     second_bias,
@@ -699,7 +756,7 @@
         + [anywhere] * 5
         + [VMEM_SPEC] * 3
         + [anywhere, VMEM_SPEC],
-        out_specs=(anywhere, VMEM_SPEC),
+        out_specs=(VMEM_SPEC, VMEM_SPEC),
         scratch_shapes=[
             pltpu.VMEM((OWN, D), BF16),
             pltpu.VMEM((HALO, D), BF16),
@@ -713,12 +770,12 @@
             pltpu.VMEM((OWN, D), F32),
             pltpu.VMEM((6, SIDE, 32, 128), F32),
             pltpu.VMEM((224, D), F32),
-            pltpu.VMEM((SIDE, SIDE, D), BF16),
             pltpu.VMEM((49, UNITS, 192), BF16),
             pltpu.VMEM((4, 4, TILES, UNITS, 128), BF16),
-            pltpu.VMEM((ROWS, 112, 384), BF16),
-            pltpu.VMEM((2, ROWS, 112, 384), BF16),
+            pltpu.VMEM((2, ROWS, 64, 384), BF16),
+            pltpu.VMEM((2, 2, ROWS, 64, 384), BF16),
             pltpu.VMEM((8, 256, 256), BF16),
+            pltpu.VMEM((COLS, 128), jnp.int32),
             pltpu.VMEM((8, 64, 128), jnp.int32),
             pltpu.VMEM((512, D), BF16),
             pltpu.VMEM((512, 512), BF16),
@@ -735,11 +792,10 @@
             dma((halo_count,)),
             dma((GATHER,)),
             dma((GATHER,)),
-            dma,
-            dma((ROWS - 1,)),
-            dma((ROWS - 1,)),
-            dma((ROWS,)),
-            dma((ROWS,)),
+            dma((6,)),
+            dma((6,)),
+            dma((8,)),
+            dma((8,)),
             dma((4,)),
             dma((4,)),
             dma((COLS,)),
@@ -748,7 +804,7 @@
             dma((ROWS - 1,)),
         ],
         compiler_params=pltpu.CompilerParams(
-            collective_id=0, has_side_effects=True, vmem_limit_bytes=62 * 1024 * 1024
+            collective_id=0, has_side_effects=True, vmem_limit_bytes=54 * 1024 * 1024
         ),
         cost_estimate=pl.CostEstimate(
             flops=27_000_000_000, bytes_accessed=34_000_000, transcendentals=6_000_000
@@ -762,7 +818,7 @@
         reduce_weight,
         first_weight,
         tiles,
-        codes,
+        shapes,
         first_bias,
         second_weight,
         second_bias,
@@ -783,12 +839,6 @@
     box_shape,
 ):
     tiles = box_tile.reshape(COLS, 128)
-    codes = (
-        (box_shape[:, 0] * 16 + box_shape[:, 1]) * 4
-        + (box_shape[:, 2] - 1) * 2
-        + (box_shape[:, 3] - 1)
-    ).reshape(COLS, 128)
-    bias = first_bias.reshape(ROWS, 4, 2, 32).transpose(0, 2, 1, 3).reshape(ROWS, 2, 128)
     features, box_features = whole(
         tokens,
         project_in,
@@ -797,10 +847,10 @@
         reduce_weight,
         first_weight.transpose(0, 2, 1),
         tiles,
-        codes,
-        bias,
+        box_shape.transpose(1, 0),
+        first_bias.reshape(8, 128),
         second_weight,
-        second_bias.reshape(ROWS, 256),
+        second_bias.reshape(8, 128),
     )
     return (features, box_features)
 

time: 122 us -> 111 us (0.910)
  Pallas kernels: 113 us -> 107 us
  local copies, waits for them, and re-layouts: 5.91 us -> 3.17 us
  other arithmetic: 1.66 us -> 0 us
    pallas_call x1, Pallas kernels: 113 us -> 107 us  [whole(): pl.pallas_call(whole_kernel, out_shape=(jax.ShapeDtypeStruct((SIDE, SIDE,...]
    reshape x3 -> x0, local copies, waits for them, and re-layouts: 2.73 us -> none  [the longest x2 1.44 us: shards(): first_bias.reshape(ROWS, 4, 2, 32).transpose(0, 2, 1, 3)]
    add x1 -> x0, other arithmetic: 1.66 us -> none  [shards(): (box_shape[:, 0] * 16 + box_shape[:, 1]) * 4 + (box_shape[:, 2] - 1) * 2]
where the time goes in v4:
time: 111 us; the launch traced here: 110 us
  Pallas kernels  107 us (96%)
  local copies, waits for them, and re-layouts  3.17 us (3%)
    pallas_call x1, Pallas kernels, whole(): pl.pallas_call(whole_kernel, out_shape=(jax.ShapeDtypeStruct((SIDE, SIDE,...  107 us
    unnamed x4, local copies, waits for them, and re-layouts  3.17 us

profile of v4, /device:TPU:0, one launch (start us, length us, event | category | flops | bytes accessed | tf_op | source)
XLA Modules:
  0.0 110.3 jit_solution(14358476116174501058)
XLA Ops:
  0.6 106.5 %whole.1 = (bf16[28,28,768]{2,1,0:T(8,128)(2,1)}, bf16[128,256]{1,0:T(8,128)(2,1)}) custom-call(bf16[28,28,768]{2,1,0:T(8,128)(2,1)} %tokens_ref.1, bf16[768,2304]{1,0:T(8,128)(2,1)} %project_in_hbm.1, bf16[768,768]{1,0:T(8,128)(2,1)} %project_out_hbm.1, bf16[768,3072]{1,0:T(8,128)(2,1)} %expand_hbm.1, bf16[3072,768]{1,0:T(8,128)(2,1)} %reduce_hbm.1, ...), custom_call_target="tpu_custom_call" | custom-call | flops 27000000512 | bytes 34000000 | tf_op jit(solution)/shard_map/whole/pallas_call | solution.py:749
  107.2 0.0 copy-start
  107.2 2.5 %copy.15 = bf16[28,28,768]{2,1,0:T(8,128)(2,1)} copy(bf16[28,28,768]{2,1,0:T(8,128)(2,1)} %get-tuple-element.4) | data formatting | bytes 2408448
  109.7 0.0 copy-done
  109.7 0.6 copy.16
Async XLA Ops:
  107.2 2.5 %copy-start = (bf16[128,256]{1,0:T(8,128)(2,1)S(1)}, bf16[128,256]{1,0:T(8,128)(2,1)}, u32[]{:S(2)}) copy-start(bf16[128,256]{1,0:T(8,128)(2,1)} %get-tuple-element.5) | copy-start | bytes 196612

commit v5 on v4

--- a/solution.py
+++ b/solution.py
@@ -284,20 +284,6 @@
                 ],
                 axis=0,
             ).astype(BF16)
-    pl.semaphore_wait(barrier, len(greeted) + COLS - 1)
-    halo_copies = [
-        remote(
-            own_ref.at[pl.ds(src, rows)],
-            halo_ref.at[pl.ds(dst, rows)],
-            halo_send.at[n],
-            halo_recv.at[n],
-            near(dr, dc),
-        )
-        for n, (src, rows, dst, dr, dc) in enumerate(HALO_COPIES)
-    ]
-    for copy in halo_copies:
-        copy.start()
-
     z, y = col // 8, lax.rem(col // 2, 4)
     loads[0].wait()
 
@@ -317,8 +303,24 @@
     whole_ref[z, y, 6 * QUADS + 1] = jnp.concatenate(
         [last[:, 128:], jnp.zeros((UNITS, 64), F32)], axis=1
     ).astype(BF16)
-    for copy in stages["own"] + stages["cross"]:
+    pl.semaphore_wait(barrier, len(greeted) + COLS - 1)
+    for copy in stages["own"]:
         copy.start()
+    halo_copies = [
+        remote(
+            own_ref.at[pl.ds(src, rows)],
+            halo_ref.at[pl.ds(dst, rows)],
+            halo_send.at[n],
+            halo_recv.at[n],
+            near(dr, dc),
+        )
+        for n, (src, rows, dst, dr, dc) in enumerate(HALO_COPIES)
+    ]
+    for copy in halo_copies:
+        copy.start()
+    for copy in stages["cross"]:
+        copy.start()
+
 
     loads[1].wait()
 
@@ -536,11 +538,16 @@
     swaps = [[to_row(half, n) for n in range(1, ROWS)] for half in range(2)]
     pairs = [[to_pair(half, n) for n in range(ROWS)] for half in range(2)]
     for half in range(2):
-        finish(((S0 + half * 112, 112), (S1 + half * 336, 112), (S2 + half * 112, 112)))
         if half == 1:
             for copy in stages["near"]:
                 copy.wait_recv()
             for copy in stages["last"]:
+                copy.start()
+        finish(((S0 + half * 112, 112), (S1 + half * 336, 112), (S2 + half * 112, 112)))
+        if half == 1:
+            for copy in stages["over"]:
+                copy.wait_recv()
+            for copy in stages["end"]:
                 copy.start()
         lax.fori_loop(half * 14, half * 14 + 14, place_row, 0)
         lax.fori_loop(half * 7, half * 7 + 7, pool, 0)
@@ -553,10 +560,6 @@
         for n in range(1, ROWS):
             swaps[half][n - 1].wait_recv()
             pairs[half][n].start()
-    for copy in stages["over"]:
-        copy.wait_recv()
-    for copy in stages["end"]:
-        copy.start()
     swaps = swaps[0] + swaps[1]
     pairs = pairs[0] + pairs[1]
     for copy in pairs:

time: 111 us -> 110 us (level)
  Pallas kernels: 107 us -> 105 us
    pallas_call x1, Pallas kernels: 107 us -> 105 us  [whole(): pl.pallas_call(whole_kernel, out_shape=(jax.ShapeDtypeStruct((SIDE, SIDE,...]
where the time goes in v5:
time: 110 us; the launch traced here: 109 us
  Pallas kernels  105 us (95%)
  local copies, waits for them, and re-layouts  3.17 us (3%)
    pallas_call x1, Pallas kernels, whole(): pl.pallas_call(whole_kernel, out_shape=(jax.ShapeDtypeStruct((SIDE, SIDE,...  105 us
    unnamed x4, local copies, waits for them, and re-layouts  3.17 us

profile of v5, /device:TPU:0, one launch (start us, length us, event | category | flops | bytes accessed | tf_op | source)
XLA Modules:
  0.0 109.2 jit_solution(14757800618115628410)
XLA Ops:
  0.6 105.4 %whole.1 = (bf16[28,28,768]{2,1,0:T(8,128)(2,1)}, bf16[128,256]{1,0:T(8,128)(2,1)}) custom-call(bf16[28,28,768]{2,1,0:T(8,128)(2,1)} %tokens_ref.1, bf16[768,2304]{1,0:T(8,128)(2,1)} %project_in_hbm.1, bf16[768,768]{1,0:T(8,128)(2,1)} %project_out_hbm.1, bf16[768,3072]{1,0:T(8,128)(2,1)} %expand_hbm.1, bf16[3072,768]{1,0:T(8,128)(2,1)} %reduce_hbm.1, ...), custom_call_target="tpu_custom_call" | custom-call | flops 27000000512 | bytes 34000000 | tf_op jit(solution)/shard_map/whole/pallas_call | solution.py:752
  106.0 0.0 copy-start
  106.0 2.5 %copy.15 = bf16[28,28,768]{2,1,0:T(8,128)(2,1)} copy(bf16[28,28,768]{2,1,0:T(8,128)(2,1)} %get-tuple-element.4) | data formatting | bytes 2408448
  108.6 0.0 copy-done
  108.6 0.6 copy.16
Async XLA Ops:
  106.0 2.5 %copy-start = (bf16[128,256]{1,0:T(8,128)(2,1)S(1)}, bf16[128,256]{1,0:T(8,128)(2,1)}, u32[]{:S(2)}) copy-start(bf16[128,256]{1,0:T(8,128)(2,1)} %get-tuple-element.5) | copy-start | bytes 196612
